TPU v7x, 32 devices: a whole 2x2x4 slice. The times are simulated.
32 devices in a mesh: cells: 8 (over y, x, core), bands: 4 (over z).
Axes of the slice: x: 2, y: 2, z: 4, core: 2. Of those that a mesh axis runs over, the one named last changes fastest.
Arguments:
- waves: bfloat16 [256, 16384], P('bands', 'cells'), may hold values from -6 to 6
- stiffness: float32 [125, 125], replicated, as said below
- cell_scale: float32 [1024], P('cells'), may hold values from 0.5 to 4
- potential: float32 [16384], P('cells'), may hold values from -2 to 2
- connect: int32 [125, 1024], P(None, 'cells'), may hold values from 0 to 3071
- live_cells: int32 [8], P('cells'), may hold values from 16 to 128, as said below
- shared: int32 [8, 2, 512], P('cells'), may hold values from 0 to 2047
- window: float32 [2], replicated, may hold values from 1 to 4
Outputs:
- filtered: float32 [256, 16384], P('bands', 'cells')
- projected: float32 [256, 256], P('cells', 'bands')
Inputs may be any that keep to these rules, and one draw needn't show every extreme that they name: `live_cells`: at least one partition has all 128 slots live. `stiffness`: symmetric positive definite.
All inputs are finite; a program needn't handle non-finite values.
Results may differ from a plain program's by a relative error of at most 0.0037.
Values may be sent and summed in bfloat16 or wider, within the bound.
A program may use at most 64 MiB of HBM per device.

v0:
```python
import math

import jax
import jax.numpy as jnp
from jax import lax
from jax.sharding import PartitionSpec as P

sigma_one = -0.5
sigma_two = 1.0 / (2.0 / sigma_one - sigma_one)


def with_halo(block, sides, width):
    for axis, dim in sides:
        count = lax.axis_size(axis)
        forward = [(i, i + 1) for i in range(count - 1)]
        backward = [(target, source) for source, target in forward]
        low = lax.ppermute(
            lax.slice_in_dim(block, block.shape[dim] - width, None, axis=dim), axis, forward
        )
        high = lax.ppermute(lax.slice_in_dim(block, 0, width, axis=dim), axis, backward)
        block = jnp.concatenate([low, block, high], axis=dim)
    return block


def local(waves, stiffness, cell_scale, potential, connect, live_cells, shared, window):
    columns, node_dev = waves.shape
    ghost = shared.shape[2]
    capacity = connect.shape[1]
    shared_rows = shared[0]
    live_count = live_cells[0]
    stiff_rounded = stiffness.astype(jnp.bfloat16)
    center = window[0]
    half_width = window[1]
    block_size = math.gcd(capacity, 128)
    block_turns = capacity // block_size
    potential_row = potential[None, :]

    def with_ghosts(owned):
        packed = jnp.concatenate([owned[:, shared_rows[0]], owned[:, shared_rows[1]]], axis=1)
        bordered = with_halo(packed, (("cells", 1),), ghost)
        return jnp.concatenate([bordered[:, :ghost], owned, bordered[:, 3 * ghost :]], axis=1)

    def assemble(totals):
        packed = jnp.concatenate([totals[:, :ghost], totals[:, ghost + node_dev :]], axis=1)
        bordered = with_halo(packed, (("cells", 1),), ghost)
        owned = totals[:, ghost : ghost + node_dev]
        return (
            owned.at[:, shared_rows[0]]
            .add(bordered[:, :ghost])
            .at[:, shared_rows[1]]
            .add(bordered[:, 3 * ghost :])
        )

    def cell_terms(extended):

        def one_block(turn, totals):
            first_cell = turn * block_size
            alive = (first_cell + jnp.arange(block_size) < live_count).astype(jnp.float32)
            weight = cell_scale * alive
            gathered = extended[:, connect]
            product = jnp.einsum(
                "ij,wjb->wib", stiff_rounded, gathered, preferred_element_type=jnp.float32
            )
            return totals.at[:, connect.reshape(-1)].add(
                (product * weight[None, None, :]).reshape(columns, -1)
            )

        empty = jnp.zeros((columns, extended.shape[1]), jnp.float32)
        return lax.fori_loop(0, block_turns, one_block, empty)

    waves32 = waves.astype(jnp.float32)
    applied_x = assemble(cell_terms(with_ghosts(waves))) + potential_row * waves32
    first_pass = ((applied_x - center * waves32) * (sigma_one / half_width)).astype(jnp.bfloat16)
    first32 = first_pass.astype(jnp.float32)
    applied_y = assemble(cell_terms(with_ghosts(first_pass))) + potential_row * first32
    filtered = (applied_y - center * first32) * (
        2.0 * sigma_two / half_width
    ) - sigma_one * sigma_two * waves32
    wave_rounded = filtered.astype(jnp.bfloat16)
    applied = assemble(cell_terms(with_ghosts(wave_rounded))) + potential_row * filtered
    apply_rounded = applied.astype(jnp.bfloat16)
    cell_count = lax.axis_size("cells")
    inverse_total = 1.0 / (node_dev * cell_count)
    partial_value = (
        jnp.einsum(
            "wn,vn->wv",
            lax.all_gather(wave_rounded, "bands", axis=0, tiled=True),
            apply_rounded,
            preferred_element_type=jnp.float32,
        )
        * inverse_total
    )
    projected = lax.psum_scatter(partial_value, "cells", scatter_dimension=0, tiled=True)
    return (filtered, projected)


def solution(mesh):
    return jax.shard_map(
        local,
        mesh=mesh,
        in_specs=(
            P("bands", "cells"),
            P(),
            P("cells"),
            P("cells"),
            P(None, "cells"),
            P("cells"),
            P("cells", None, None),
            P(),
        ),
        out_specs=(P("bands", "cells"), P("cells", "bands")),
        check_vma=False,
    )
```

profile of v0, /device:TPU:0, one launch (start us, length us, event | category | flops | bytes accessed | tf_op | source)
XLA Modules:
  0.0 611.2 jit_solution(1854243036892505249)
XLA Ops:
  7.2 0.8 compare_select_fusion.3
  8.0 0.6 copy-done.4
  8.6 1.2 copy.32
  9.8 1.3 gather_fusion
  11.2 2.4 collective-permute-start
  13.6 1.3 gather_fusion.1
  14.9 1.3 collective-permute-start.1
  16.2 0.9 fusion.30
  18.0 0.6 fusion.43
  19.3 1.0 collective-permute-done.1
  20.4 33.1 %gather_fusion.2 = bf16[16000,64]{1,0:T(8,128)(2,1)} fusion(bf16[64,3072]{0,1:T(8,128)(2,1)S(1)} %pad_maximum_fusion, s32[16384]{0:T(1024)S(1)} %pad_clamp_fusion), kind=kCustom, calls=%fused_computation.2 | custom fusion | bytes 4160000 | tf_op jit(solution)/shard_map/while/body/eval_jaxpr/gather | solution.py:60
  53.5 7.4 %copy.35 = bf16[125,128,64]{0,1,2:T(8,128)(2,1)S(1)} copy(bf16[125,128,64]{2,1,0:T(8,128)(2,1)} %bitcast.96) | data formatting | bytes 4096000 | tf_op jit(solution)/shard_map/while/body/eval_jaxpr/gather | solution.py:60
  60.9 2.7 multiply_bitcast_fusion.2
  63.6 5.7 copy.36
  69.2 6.5 %copy.57 = f32[8,8,125,128]{3,1,2,0:T(8,128)} copy(f32[8,8,125,128]{3,2,1,0:T(8,128)} %bitcast.89) | data formatting | bytes 8192000
  75.7 6.8 %copy.37 = f32[16000,64]{1,0:T(8,128)} copy(f32[16000,64]{0,1:T(8,128)} %bitcast.92) | data formatting | bytes 8192000 | tf_op jit(solution)/shard_map/while/body/eval_jaxpr/reshape | solution.py:65
  82.5 88.3 %scatter_custom_fusion = f32[64,3072]{0,1:T(8,128)S(1)} fusion(s32[16000]{0:T(1024)S(1)} %fusion.31, f32[16000,64]{1,0:T(8,128)} %copy.37, f32[]{:T(128)} %constant.22.clone.1), kind=kCustom, calls=%fused_computation.49 | custom fusion | flops 1024000 | bytes 786944 | tf_op jit(solution)/shard_map/while/body/eval_jaxpr/scatter-add | solution.py:64
  170.9 0.7 fusion.42
  171.6 6.1 %collective-permute-start.2 = (f32[64,512]{0,1:T(8,128)S(1)}, f32[64,512]{0,1:T(8,128)}, u32[]{:S(2)}, u32[]{:S(2)}) collective-permute-start(f32[64,512]{0,1:T(8,128)S(1)} %get-tuple-element.71), channel_id=1, source_target_pairs={{0,4},{4,8},{8,12},{12,16},{16,20},{20,24},{24,28},{1,5},{5,9},{9,... | collective-permute-start | bytes 393224 | tf_op jit(solution)/shard_map/ppermute | solution.py:17
  177.7 1.3 collective-permute-start.3
  179.0 0.3 fusion.7
  179.4 4.4 scatter_custom_fusion.1
  183.8 3.8 scatter_custom_fusion.2
  187.6 0.7 fusion.10
  188.3 1.3 gather_fusion.3
  189.7 1.3 gather_fusion.4
  191.0 4.3 collective-permute-start.4
  195.3 1.3 collective-permute-start.5
  197.3 2.4 collective-permute-done.5
  199.8 33.1 %gather_fusion.5 = bf16[16000,64]{1,0:T(8,128)(2,1)} fusion(bf16[64,3072]{0,1:T(8,128)(2,1)S(1)} %pad_maximum_fusion.1, s32[16384]{0:T(1024)S(1)} %pad_clamp_fusion), kind=kCustom, calls=%fused_computation.5 | custom fusion | bytes 4160000 | tf_op jit(solution)/shard_map/while/body/eval_jaxpr/gather | solution.py:60
  232.9 7.3 %copy.39 = bf16[125,128,64]{0,1,2:T(8,128)(2,1)S(1)} copy(bf16[125,128,64]{2,1,0:T(8,128)(2,1)} %bitcast.97) | data formatting | bytes 4096000 | tf_op jit(solution)/shard_map/while/body/eval_jaxpr/gather | solution.py:60
  240.3 2.7 multiply_bitcast_fusion.1
  242.9 5.7 copy.40
  248.6 6.5 %copy.56 = f32[8,8,125,128]{3,1,2,0:T(8,128)} copy(f32[8,8,125,128]{3,2,1,0:T(8,128)} %bitcast.90) | data formatting | bytes 8192000
  255.1 6.8 %copy.41 = f32[16000,64]{1,0:T(8,128)} copy(f32[16000,64]{0,1:T(8,128)} %bitcast.93) | data formatting | bytes 8192000 | tf_op jit(solution)/shard_map/while/body/eval_jaxpr/reshape | solution.py:65
  261.9 88.3 %scatter_custom_fusion.3 = f32[64,3072]{0,1:T(8,128)S(1)} fusion(s32[16000]{0:T(1024)} %copy-done.3, f32[16000,64]{1,0:T(8,128)} %copy.41, f32[]{:T(128)} %constant.22.clone.1), kind=kCustom, calls=%fused_computation.47 | custom fusion | flops 1024000 | bytes 786944 | tf_op jit(solution)/shard_map/while/body/eval_jaxpr/scatter-add | solution.py:64
  350.3 6.3 %collective-permute-start.6 = (f32[64,512]{0,1:T(8,128)S(1)}, f32[64,512]{0,1:T(8,128)S(1)}, u32[]{:S(2)}, u32[]{:S(2)}) collective-permute-start(f32[64,512]{0,1:T(8,128)S(1)} %get-tuple-element.69), channel_id=1, source_target_pairs={{0,4},{4,8},{8,12},{12,16},{16,20},{20,24},{24,28},{1,5},{5,9},{9,... | collective-permute-start | bytes 393224 | tf_op jit(solution)/shard_map/ppermute | solution.py:17
  356.6 1.3 collective-permute-start.7
  357.9 1.3 fusion.3
  359.2 13.7 %scatter_custom_fusion.4 = f32[64,2048]{0,1:T(8,128)} fusion(f32[64,2048]{0,1:T(8,128)} %fusion.3, s32[512]{0:T(512)} %bitcast.111, f32[64,512]{0,1:T(8,128)S(1)} %collective-permute-done.6), kind=kCustom, calls=%fused_computation.59 | custom fusion | flops 32768 | bytes 655360 | tf_op jit(solution)/shard_map/scatter-add | solution.py:49
  372.9 5.3 scatter_custom_fusion.5
  378.2 2.1 fusion.38
  380.3 1.3 gather_fusion.6
  381.6 1.3 gather_fusion.7
  383.0 3.0 collective-permute-start.8
  386.0 1.3 collective-permute-start.9
  387.3 0.9 copy.42
  388.3 3.8 collective-permute-done.9
  392.2 33.1 %gather_fusion.8 = bf16[16000,64]{1,0:T(8,128)(2,1)} fusion(bf16[64,3072]{0,1:T(8,128)(2,1)S(1)} %pad_maximum_fusion.2, s32[16384]{0:T(1024)S(1)} %pad_clamp_fusion), kind=kCustom, calls=%fused_computation.8 | custom fusion | bytes 4160000 | tf_op jit(solution)/shard_map/while/body/eval_jaxpr/gather | solution.py:60
  425.3 8.0 %copy.43 = bf16[125,128,64]{0,1,2:T(8,128)(2,1)} copy(bf16[125,128,64]{2,1,0:T(8,128)(2,1)} %bitcast.95) | data formatting | bytes 4096000 | tf_op jit(solution)/shard_map/while/body/eval_jaxpr/gather | solution.py:60
  433.3 4.2 multiply_bitcast_fusion
  437.5 5.7 copy.44
  443.2 6.4 %copy.55 = f32[8,8,125,128]{3,1,2,0:T(8,128)} copy(f32[8,8,125,128]{3,2,1,0:T(8,128)} %bitcast.91) | data formatting | bytes 8192000
  449.6 6.8 %copy.45 = f32[16000,64]{1,0:T(8,128)} copy(f32[16000,64]{0,1:T(8,128)} %bitcast.94) | data formatting | bytes 8192000 | tf_op jit(solution)/shard_map/while/body/eval_jaxpr/reshape | solution.py:65
  456.4 89.2 %scatter_custom_fusion.6 = f32[64,3072]{0,1:T(8,128)} fusion(s32[16000]{0:T(1024)} %copy-done.3, f32[16000,64]{1,0:T(8,128)} %copy.45, f32[]{:T(128)} %constant.22.clone.1), kind=kCustom, calls=%fused_computation.45 | custom fusion | flops 1024000 | bytes 786944 | tf_op jit(solution)/shard_map/while/body/eval_jaxpr/scatter-add | solution.py:64
  545.6 1.1 fusion.40
  546.7 6.1 collective-permute-start.10
  552.8 1.5 collective-permute-start.11
  554.3 1.6 slice_add_fusion
  555.9 3.8 scatter_custom_fusion.7
  559.8 3.8 scatter_custom_fusion.8
  563.6 2.3 convolution_multiply_fusion
  565.9 1.1 copy.46
  567.1 37.1 %reduce-scatter.2.cloned.1.call-done = f32[32,64]{1,0:T(8,128)} async-done(((f32[256,64]{1,0:T(8,128)}), f32[32,64]{1,0:T(8,128)}) %reduce-scatter.2.cloned.1.call-update) | async-done | bytes 8208 | tf_op jit(solution)/shard_map/reduce_scatter | solution.py:93
  (44 shorter events, 0.9 us)
Async XLA Ops:
  7.2 10.6 %copy-start.1 = (s32[125,128]{1,0:T(8,128)S(1)}, s32[125,128]{1,0:T(8,128)}, u32[]{:S(2)}) copy-start(s32[125,128]{1,0:T(8,128)} %param.12) | copy-start | bytes 192004
  7.2 10.8 %copy-start.10 = (f32[128]{0:T(128)S(1)}, f32[128]{0:T(128)}, u32[]{:S(2)}) copy-start(f32[128]{0:T(128)} %param.10) | copy-start | bytes 1540
  7.2 10.8 %copy-start.9 = (f32[2]{0:T(128)S(1)}, f32[2]{0:T(128)}, u32[]{:S(2)}) copy-start(f32[2]{0:T(128)} %param.15) | copy-start | bytes 28
  7.2 556.4 %all-gather.2.cloned.1.call-start = ((), (), s32[]{:S(2)}) async-start(), calls=%async_computation.1 | async-start | bytes 1310720 | tf_op jit(solution)/shard_map/all_gather | solution.py:87
  8.0 0.6 copy-start.4
  8.0 6.9 %copy-start.5 = (s32[512,1]{0,1:T(1,128)}, s32[512,1]{0,1:T(1,128)S(1)}, u32[]{:S(2)}) copy-start(s32[512,1]{0,1:T(1,128)S(1)} %get-tuple-element.81) | copy-start | bytes 6148
  11.2 8.1 %collective-permute-start = (bf16[64,512]{0,1:T(8,128)(2,1)S(1)}, bf16[64,512]{0,1:T(8,128)(2,1)S(1)}, u32[]{:S(2)}, u32[]{:S(2)}) collective-permute-start(bf16[64,512]{0,1:T(8,128)(2,1)S(1)} %bitcast.100), channel_id=1, source_target_pairs={{0,4},{4,8},{8,12},{12,16},{16,20},{20,24},{24,28},{1,5},{5,9},{9,... | collective-permute-start | bytes 196616 | tf_op jit(solution)/shard_map/ppermute | solution.py:17
  14.9 5.3 collective-permute-start.1
  17.9 64.6 %copy-start.3 = (s32[16000]{0:T(1024)}, s32[16000]{0:T(1024)S(1)}, u32[]{:S(2)}) copy-start(s32[16000]{0:T(1024)S(1)} %fusion.31) | copy-start | bytes 192004
  18.0 42.9 %copy-start.6 = (f32[128]{0:T(128)}, f32[128]{0:T(128)S(1)}, u32[]{:S(2)}) copy-start(f32[128]{0:T(128)S(1)} %compare_select_fusion.4) | copy-start | bytes 1540
  53.5 7.4 %copy-start = (f32[125,125]{1,0:T(8,128)S(1)}, f32[125,125]{1,0:T(8,128)}, u32[]{:S(2)}) copy-start(f32[125,125]{1,0:T(8,128)} %param.9) | copy-start | bytes 187504
  82.5 96.5 %copy-start.2 = (f32[2048]{0:T(1024)S(1)}, f32[2048]{0:T(1024)}, u32[]{:S(2)}) copy-start(f32[2048]{0:T(1024)} %param.11) | copy-start | bytes 24580
  171.6 7.8 %collective-permute-start.2 = (f32[64,512]{0,1:T(8,128)S(1)}, f32[64,512]{0,1:T(8,128)}, u32[]{:S(2)}, u32[]{:S(2)}) collective-permute-start(f32[64,512]{0,1:T(8,128)S(1)} %get-tuple-element.71), channel_id=1, source_target_pairs={{0,4},{4,8},{8,12},{12,16},{16,20},{20,24},{24,28},{1,5},{5,9},{9,... | collective-permute-start | bytes 393224 | tf_op jit(solution)/shard_map/ppermute | solution.py:17
  177.7 6.0 collective-permute-start.3
  191.0 6.3 %collective-permute-start.4 = (bf16[64,512]{0,1:T(8,128)(2,1)S(1)}, bf16[64,512]{0,1:T(8,128)(2,1)S(1)}, u32[]{:S(2)}, u32[]{:S(2)}) collective-permute-start(bf16[64,512]{0,1:T(8,128)(2,1)S(1)} %bitcast.104), channel_id=1, source_target_pairs={{0,4},{4,8},{8,12},{12,16},{16,20},{20,24},{24,28},{1,5},{5,9},{9,... | collective-permute-start | bytes 196616 | tf_op jit(solution)/shard_map/ppermute | solution.py:17
  195.3 4.3 collective-permute-start.5
  232.9 7.3 %copy-start.7 = (f32[128]{0:T(128)S(1)}, f32[128]{0:T(128)}, u32[]{:S(2)}) copy-start(f32[128]{0:T(128)} %copy-done.6) | copy-start | bytes 1540
  350.3 8.9 %collective-permute-start.6 = (f32[64,512]{0,1:T(8,128)S(1)}, f32[64,512]{0,1:T(8,128)S(1)}, u32[]{:S(2)}, u32[]{:S(2)}) collective-permute-start(f32[64,512]{0,1:T(8,128)S(1)} %get-tuple-element.69), channel_id=1, source_target_pairs={{0,4},{4,8},{8,12},{12,16},{16,20},{20,24},{24,28},{1,5},{5,9},{9,... | collective-permute-start | bytes 393224 | tf_op jit(solution)/shard_map/ppermute | solution.py:17
  356.6 16.3 %collective-permute-start.7 = (f32[64,512]{0,1:T(8,128)S(1)}, f32[64,512]{0,1:T(8,128)S(1)}, u32[]{:S(2)}, u32[]{:S(2)}) collective-permute-start(f32[64,512]{0,1:T(8,128)S(1)} %get-tuple-element.68), channel_id=1, source_target_pairs={{4,0},{8,4},{12,8},{16,12},{20,16},{24,20},{28,24},{5,1},{9,5},{13... | collective-permute-start | bytes 393224 | tf_op jit(solution)/shard_map/ppermute | solution.py:20
  383.0 5.3 collective-permute-start.8
  386.0 6.1 collective-permute-start.9
  388.2 215.9 %reduce-scatter.2.cloned.1.call-start = ((), (), s32[]{:S(2)}) async-start(), calls=%async_computation.2 | async-start | bytes 147456 | tf_op jit(solution)/shard_map/reduce_scatter | solution.py:93
  425.3 8.0 %copy-start.8 = (f32[128]{0:T(128)S(1)}, f32[128]{0:T(128)}, u32[]{:S(2)}) copy-start(f32[128]{0:T(128)} %copy-done.6) | copy-start | bytes 1540
  546.7 9.2 %collective-permute-start.10 = (f32[64,512]{0,1:T(8,128)S(1)}, f32[64,512]{0,1:T(8,128)S(1)}, u32[]{:S(2)}, u32[]{:S(2)}) collective-permute-start(f32[64,512]{0,1:T(8,128)S(1)} %get-tuple-element.67), channel_id=1, source_target_pairs={{0,4},{4,8},{8,12},{12,16},{16,20},{20,24},{24,28},{1,5},{5,9},{9,... | collective-permute-start | bytes 393224 | tf_op jit(solution)/shard_map/ppermute | solution.py:17
  552.8 6.9 %collective-permute-start.11 = (f32[64,512]{0,1:T(8,128)S(1)}, f32[64,512]{0,1:T(8,128)S(1)}, u32[]{:S(2)}, u32[]{:S(2)}) collective-permute-start(f32[64,512]{0,1:T(8,128)S(1)} %get-tuple-element.66), channel_id=1, source_target_pairs={{4,0},{8,4},{12,8},{16,12},{20,16},{24,20},{28,24},{5,1},{9,5},{13... | collective-permute-start | bytes 393224 | tf_op jit(solution)/shard_map/ppermute | solution.py:20
Sparse Core Ops, SparseCore 0:
  388.3 35.1 all-gather.1
  566.1 38.0 reduce-scatter.1
where the time goes:
time: 617 us; the launch traced here: 611 us
  other arithmetic  309 us (50%)
  local copies, waits for them, and re-layouts  193 us (31%)
  waiting for transfers between devices  44.3 us (7%)
  starting transfers between devices  36.2 us (6%)
  between operations  16.7 us (3%)
  matrix products  11.9 us (2%)
    scatter-add x3, other arithmetic, one_block(): totals.at[:, connect.reshape(-1)]  266 us
    gather x6, local copies, waits for them, and re-layouts, one_block(): gathered = extended[:, connect]  122 us
    reduce_scatter x1, waiting for transfers between devices, local(): lax.psum_scatter(partial_value, 'cells', scatter_dimension=0, tiled=True)  37.1 us
    scatter-add x6, other arithmetic, assemble(): return owned.at[:, shared_rows[0]].add(bordered[:, :ghost]).at[:, shared_...  34.9 us
    ppermute x6, starting transfers between devices, with_halo(): lax.ppermute(lax.slice_in_dim(block, block.shape[dim] - width, None, axis...  28.2 us
    unnamed x27, local copies, waits for them, and re-layouts  22.3 us
    reshape x3, local copies, waits for them, and re-layouts, one_block(): (product * weight[None, None, :]).reshape(columns, -1)  20.4 us
    mul x3, local copies, waits for them, and re-layouts, one_block(): product * weight[None, None, :]  17 us
  transfers between devices with their start and end apart: 14, of which 4 were waited for; matrix products, arithmetic and copies ran while one was open for 31% of the time, Pallas kernels for 0%

commit v1 on v0

v1 whole, which is shorter than its diff:
```python
import functools
import math

import jax
import jax.numpy as jnp
from jax import lax
from jax.experimental import pallas as pl
from jax.experimental.pallas import tpu as pltpu
from jax.sharding import PartitionSpec as P

sigma_one = -0.5
sigma_two = 1.0 / (2.0 / sigma_one - sigma_one)

LANES = 128
WAYS = 4


def cell_kernel(
    nodes, capacity, columns, connect, scale, live, stiff, ext, out, x0, x1, p0, p1, *sums
):
    lows, highs = sums[:WAYS], sums[WAYS:]
    rows = ext.shape[0]
    chunk = math.gcd(rows, 256)

    @pl.loop(0, rows // chunk)
    def _(step):
        at = pl.ds(pl.multiple_of(step * chunk, chunk), chunk)
        for total in sums:
            total[at, :] = jnp.zeros((chunk, LANES), jnp.float32)

    low_lanes = lax.broadcasted_iota(jnp.int32, (1, LANES), 1) < columns
    live_count = live[0]
    pairs = (live_count + 1) // 2
    last = capacity // 2 - 1

    def cells_of(pair):
        first = jnp.minimum(pair, last) * 2
        return first, first + 1

    def gather(pair, x):
        first, second = cells_of(pair)
        for j in range(nodes):
            a = connect[j, first]
            b = connect[j, second]
            x[j : j + 1, :] = jnp.where(low_lanes, ext[pl.ds(a, 1), :], ext[pl.ds(b, 1), :])

    def multiply(pair, x, p):
        first, second = cells_of(pair)
        low = jnp.where(pair * 2 < live_count, scale[first], 0.0)
        high = jnp.where(pair * 2 + 1 < live_count, scale[second], 0.0)
        weight = jnp.where(low_lanes, low, high)
        p[...] = weight * jnp.dot(
            stiff[...], x[...].astype(jnp.bfloat16), preferred_element_type=jnp.float32
        )

    def scatter(pair, p):
        first, second = cells_of(pair)
        for begin in range(0, nodes, WAYS):
            todo = []
            for way in range(min(WAYS, nodes - begin)):
                j = begin + way
                term = p[j : j + 1, :]
                for sums_of, cell in ((lows, first), (highs, second)):
                    at = pl.ds(connect[j, cell], 1)
                    todo.append((sums_of[way], at, sums_of[way][at, :] + term))
            for total, at, value in todo:
                total[at, :] = value

    x0[...] = jnp.zeros_like(x0)
    x1[...] = jnp.zeros_like(x1)
    gather(0, x0)
    multiply(0, x0, p0)
    gather(1, x1)

    @pl.loop(0, (pairs + 1) // 2)
    def _(turn):
        pair = turn * 2
        scatter(pair, p0)
        multiply(pair + 1, x1, p1)
        gather(pair + 2, x0)
        scatter(pair + 1, p1)
        multiply(pair + 2, x0, p0)
        gather(pair + 3, x1)

    @pl.loop(0, rows // chunk)
    def _(step):
        at = pl.ds(pl.multiple_of(step * chunk, chunk), chunk)
        low = lows[0][at, :]
        high = highs[0][at, :]
        for way in range(1, WAYS):
            low += lows[way][at, :]
            high += highs[way][at, :]
        out[at, :] = low[:, :columns] + high[:, columns : 2 * columns]


def cell_sums(ext, stiff, connect, scale, live):
    rows, columns = ext.shape
    assert 2 * columns == LANES
    nodes, capacity = connect.shape
    depth = stiff.shape[0]
    vmem = pl.BlockSpec(memory_space=pltpu.VMEM)
    smem = pl.BlockSpec(memory_space=pltpu.SMEM)
    wide = jnp.concatenate([ext, ext], axis=1).astype(jnp.float32)
    return pl.pallas_call(
        functools.partial(cell_kernel, nodes, capacity, columns),
        out_shape=jax.ShapeDtypeStruct((rows, columns), jnp.float32),
        in_specs=[smem, smem, smem, vmem, vmem],
        out_specs=vmem,
        scratch_shapes=[pltpu.VMEM((depth, LANES), jnp.float32)] * 4
        + [pltpu.VMEM((rows, LANES), jnp.float32)] * (2 * WAYS),
        compiler_params=pltpu.CompilerParams(vmem_limit_bytes=40 * 1024 * 1024),
    )(connect, scale, live, stiff, wide)


def local(waves, stiffness, cell_scale, potential, connect, live_cells, shared, window):
    columns, node_dev = waves.shape
    ghost = shared.shape[2]
    low_nodes, high_nodes = shared[0, 0], shared[0, 1]
    nodes = connect.shape[0]
    depth = -(-nodes // LANES) * LANES
    stiff = jnp.pad(stiffness, ((0, depth - nodes), (0, depth - nodes))).astype(jnp.bfloat16)
    center = window[0]
    half_width = window[1]
    potential_col = potential[:, None]
    count = lax.axis_size("cells")
    forward = [(i, i + 1) for i in range(count - 1)]
    backward = [(i + 1, i) for i in range(count - 1)]

    def apply(owned):
        lower = lax.ppermute(owned[high_nodes], "cells", forward)
        upper = lax.ppermute(owned[low_nodes], "cells", backward)
        ext = jnp.concatenate([lower, owned, upper], axis=0)
        totals = cell_sums(ext, stiff, connect, cell_scale, live_cells)
        from_lower = lax.ppermute(totals[ghost + node_dev :], "cells", forward)
        from_upper = lax.ppermute(totals[:ghost], "cells", backward)
        return (
            totals[ghost : ghost + node_dev]
            .at[jnp.concatenate([low_nodes, high_nodes])]
            .add(jnp.concatenate([from_lower, from_upper], axis=0))
        )

    start = waves.T
    start32 = start.astype(jnp.float32)
    applied_x = apply(start) + potential_col * start32
    first_pass = ((applied_x - center * start32) * (sigma_one / half_width)).astype(jnp.bfloat16)
    first32 = first_pass.astype(jnp.float32)
    applied_y = apply(first_pass) + potential_col * first32
    filtered = (applied_y - center * first32) * (
        2.0 * sigma_two / half_width
    ) - sigma_one * sigma_two * start32
    wave_rounded = filtered.astype(jnp.bfloat16)
    gathered = lax.all_gather(wave_rounded, "bands", axis=1, tiled=True)
    applied = apply(wave_rounded) + potential_col * filtered
    apply_rounded = applied.astype(jnp.bfloat16)
    inverse_total = 1.0 / (node_dev * count)
    partial_value = (
        jnp.einsum("nw,nv->wv", gathered, apply_rounded, preferred_element_type=jnp.float32)
        * inverse_total
    )
    projected = lax.psum_scatter(partial_value, "cells", scatter_dimension=0, tiled=True)
    return (filtered.T, projected)


def solution(mesh):
    return jax.shard_map(
        local,
        mesh=mesh,
        in_specs=(
            P("bands", "cells"),
            P(),
            P("cells"),
            P("cells"),
            P(None, "cells"),
            P("cells"),
            P("cells", None, None),
            P(),
        ),
        out_specs=(P("bands", "cells"), P("cells", "bands")),
        check_vma=False,
    )
```

time: 617 us -> 258 us (0.42)
  other arithmetic: 309 us -> 24.6 us
  local copies, waits for them, and re-layouts: 193 us -> 13 us
  waiting for transfers between devices: 44.3 us -> 113 us
  Pallas kernels: 0 us -> 48.1 us
  matrix products: 11.9 us -> 2.32 us
    scatter-add x9 -> x3, other arithmetic: 301 us -> 18.7 us  [apply(): return totals[ghost:ghost + node_dev].at[jnp.concatenate([low_nodes, high...]
    gather x12 -> x6, local copies, waits for them, and re-layouts: 130 us -> 8.05 us  [the longest x3 4.03 us: apply(): upper = lax.ppermute(owned[low_nodes], 'cells', backward)]
    ppermute x12, waiting for transfers between devices: 7.18 us -> 76.6 us  [the longest x3 71.4 us: apply(): from_upper = lax.ppermute(totals[:ghost], 'cells', backward)]
    pallas_call x0 -> x3, Pallas kernels: none -> 48.1 us  [cell_sums(): pl.pallas_call(functools.partial(cell_kernel, nodes, capacity, columns),...]
    reshape x3 -> x0, local copies, waits for them, and re-layouts: 20.4 us -> none  [one_block(): (product * weight[None, None, :]).reshape(columns, -1)]
    unnamed x27 -> x16, local copies, waits for them, and re-layouts: 22.3 us -> 3.35 us
    mul x3 -> x0, local copies, waits for them, and re-layouts: 17 us -> none  [one_block(): product * weight[None, None, :]]
    dot_general x4 -> x1, matrix products: 11.9 us -> 2.32 us  [local(): jnp.einsum('nw,nv->wv', gathered, apply_rounded, preferred_element_type=j...]
  transfers between devices with their start and end apart: 14 -> 14, of which waited for: 4 -> 7; matrix products, arithmetic and copies ran while one was open for 31% -> 5% of each run, Pallas kernels for 0% -> 6%
where the time goes in v1:
time: 258 us; the launch traced here: 257 us
  waiting for transfers between devices  113 us (44%)
  Pallas kernels  48.1 us (19%)
  starting transfers between devices  39.3 us (15%)
  other arithmetic  24.6 us (10%)
  between operations  16.5 us (6%)
  local copies, waits for them, and re-layouts  13 us (5%)
    ppermute x3, waiting for transfers between devices, apply(): from_upper = lax.ppermute(totals[:ghost], 'cells', backward)  71.4 us
    pallas_call x3, Pallas kernels, cell_sums(): pl.pallas_call(functools.partial(cell_kernel, nodes, capacity, columns),...  48.1 us
    reduce_scatter x1, waiting for transfers between devices, local(): lax.psum_scatter(partial_value, 'cells', scatter_dimension=0, tiled=True)  36.2 us
    scatter-add x3, other arithmetic, apply(): return totals[ghost:ghost + node_dev].at[jnp.concatenate([low_nodes, high...  18.7 us
    ppermute x3, starting transfers between devices, apply(): from_lower = lax.ppermute(totals[ghost + node_dev:], 'cells', forward)  15.8 us
    ppermute x3, starting transfers between devices, apply(): lower = lax.ppermute(owned[high_nodes], 'cells', forward)  15.7 us
    ppermute x3, waiting for transfers between devices, apply(): upper = lax.ppermute(owned[low_nodes], 'cells', backward)  5.2 us
  transfers between devices with their start and end apart: 14, of which 7 were waited for; matrix products, arithmetic and copies ran while one was open for 5% of the time, Pallas kernels for 6%

profile of v1, /device:TPU:0, one launch (start us, length us, event | category | flops | bytes accessed | tf_op | source)
XLA Modules:
  0.0 256.7 jit_solution(2551400821739019857)
XLA Ops:
  7.2 0.0 copy-start.5
  7.2 0.0 copy-start.4
  7.2 0.0 all-gather.2.cloned.1.call-start
  7.2 1.2 copy.14
  8.5 0.8 compare_select_fusion.2
  9.3 1.3 gather_fusion
  10.6 2.4 collective-permute-start
  13.0 0.0 copy-start
  13.0 0.0 copy-start.1
  13.0 1.3 gather_fusion.1
  14.4 1.3 collective-permute-start.1
  16.4 0.6 fusion.26
  17.7 0.0 collective-permute-done
  17.7 2.0 collective-permute-done.1
  19.7 0.4 maximum_convert_fusion.ext
  20.1 0.0 copy-done
  20.1 0.0 copy-done.1
  20.1 0.0 copy-start.3
  20.1 16.0 %shard_map.95 = f32[3072,64]{1,0:T(8,128)S(1)} custom-call(s32[125,128]{1,0:T(8,128)S(1)} %copy-done, f32[128]{0:T(128)S(1)} %copy-done.1, s32[1]{0:T(128)S(6)} %copy.20.live, bf16[128,128]{1,0:T(8,128)(2,1)S(1)} %pad.5.stiff, f32[3072,128]{1,0:T(8,128)S(1)} %maximum_convert_fusion.ext), custom_call_target="tpu_custom_call" | custom-call | tf_op jit(solution)/shard_map/pallas_call | solution.py:104
  36.2 5.5 %collective-permute-start.2 = (f32[512,64]{1,0:T(8,128)S(1)}, f32[512,64]{1,0:T(8,128)S(1)}, u32[]{:S(2)}, u32[]{:S(2)}) collective-permute-start(f32[512,64]{1,0:T(8,128)S(1)} %get-tuple-element.14), channel_id=1, source_target_pairs={{0,4},{4,8},{8,12},{12,16},{16,20},{20,24},{24,28},{1,5},{5,9},{9,... | collective-permute-start | bytes 393224 | tf_op jit(solution)/shard_map/ppermute | solution.py:134
  41.7 1.3 collective-permute-start.3
  43.0 0.3 fusion.4
  43.3 0.0 collective-permute-done.2
  43.3 23.9 %collective-permute-done.3 = f32[512,64]{1,0:T(8,128)S(1)} collective-permute-done((f32[512,64]{1,0:T(8,128)S(1)}, f32[512,64]{1,0:T(8,128)S(1)}, u32[]{:S(2)}, u32[]{:S(2)}) %collective-permute-start.3) | collective-permute-done | bytes 131104 | tf_op jit(solution)/shard_map/ppermute | solution.py:135
  67.2 6.2 %scatter_custom_fusion = f32[2048,64]{1,0:T(8,128)S(1)} fusion(f32[2048,64]{1,0:T(8,128)S(1)} %fusion.4, s32[1024]{0:T(1024)S(1)} %bitcast.27, f32[512,64]{1,0:T(8,128)S(1)} %collective-permute-done.3, f32[]{:T(128)} %constant.24, f32[512,64]{1,0:T(8,128)S(1)} %collective-permute-done.2), kind=kCustom, calls=%fused_computation.27 | custom fusion | flops 131072 | bytes 1048580 | tf_op jit(solution)/shard_map/scatter-add | solution.py:139
  73.4 0.8 fusion.7
  74.3 1.3 gather_fusion.2
  75.6 1.3 gather_fusion.3
  77.0 6.7 %collective-permute-start.4 = (bf16[512,64]{1,0:T(8,128)(2,1)S(1)}, bf16[512,64]{1,0:T(8,128)(2,1)S(1)}, u32[]{:S(2)}, u32[]{:S(2)}) collective-permute-start(bf16[512,64]{1,0:T(8,128)(2,1)S(1)} %gather_fusion.2), channel_id=1, source_target_pairs={{0,4},{4,8},{8,12},{12,16},{16,20},{20,24},{24,28},{1,5},{5,9},{9,... | collective-permute-start | bytes 196616 | tf_op jit(solution)/shard_map/ppermute | solution.py:130
  83.6 1.3 collective-permute-start.5
  85.6 0.0 collective-permute-done.4
  85.6 1.2 collective-permute-done.5
  86.9 0.4 maximum_convert_fusion.1.ext
  87.3 16.0 %shard_map.96 = f32[3072,64]{1,0:T(8,128)S(1)} custom-call(s32[125,128]{1,0:T(8,128)S(1)} %copy-done, f32[128]{0:T(128)S(1)} %copy-done.1, s32[1]{0:T(128)S(6)} %copy.20.live, bf16[128,128]{1,0:T(8,128)(2,1)S(1)} %pad.5.stiff, f32[3072,128]{1,0:T(8,128)S(1)} %maximum_convert_fusion.1.ext), custom_call_target="tpu_custom_call" | custom-call | tf_op jit(solution)/shard_map/pallas_call | solution.py:104
  103.3 5.0 %collective-permute-start.6 = (f32[512,64]{1,0:T(8,128)S(1)}, f32[512,64]{1,0:T(8,128)S(1)}, u32[]{:S(2)}, u32[]{:S(2)}) collective-permute-start(f32[512,64]{1,0:T(8,128)S(1)} %get-tuple-element.12), channel_id=1, source_target_pairs={{0,4},{4,8},{8,12},{12,16},{16,20},{20,24},{24,28},{1,5},{5,9},{9,... | collective-permute-start | bytes 393224 | tf_op jit(solution)/shard_map/ppermute | solution.py:134
  108.3 1.3 collective-permute-start.7
  109.6 0.3 fusion
  110.0 0.0 collective-permute-done.6
  110.0 23.9 %collective-permute-done.7 = f32[512,64]{1,0:T(8,128)S(1)} collective-permute-done((f32[512,64]{1,0:T(8,128)S(1)}, f32[512,64]{1,0:T(8,128)S(1)}, u32[]{:S(2)}, u32[]{:S(2)}) %collective-permute-start.7) | collective-permute-done | bytes 131104 | tf_op jit(solution)/shard_map/ppermute | solution.py:135
  133.9 6.4 %scatter_custom_fusion.1 = f32[2048,64]{1,0:T(8,128)S(1)} fusion(f32[2048,64]{1,0:T(8,128)S(1)} %fusion, s32[1024]{0:T(1024)S(1)} %bitcast.28, f32[512,64]{1,0:T(8,128)S(1)} %collective-permute-done.7, f32[]{:T(128)} %constant.24, f32[512,64]{1,0:T(8,128)S(1)} %collective-permute-done.6), kind=kCustom, calls=%fused_computation.31 | custom fusion | flops 131072 | bytes 1048580 | tf_op jit(solution)/shard_map/scatter-add | solution.py:139
  140.3 1.0 copy-done.2
  141.3 2.2 fusion.21
  143.4 0.9 copy.15
  144.3 0.0 all-gather.2.cloned.1.call-update
  144.4 0.0 reduce-scatter.2.cloned.1.call-start
  144.4 1.3 gather_fusion.4
  145.8 1.3 gather_fusion.5
  147.1 6.7 %collective-permute-start.8 = (bf16[512,64]{1,0:T(8,128)(2,1)S(1)}, bf16[512,64]{1,0:T(8,128)(2,1)S(1)}, u32[]{:S(2)}, u32[]{:S(2)}) collective-permute-start(bf16[512,64]{1,0:T(8,128)(2,1)S(1)} %gather_fusion.4), channel_id=1, source_target_pairs={{0,4},{4,8},{8,12},{12,16},{16,20},{20,24},{24,28},{1,5},{5,9},{9,... | collective-permute-start | bytes 196616 | tf_op jit(solution)/shard_map/ppermute | solution.py:130
  153.8 1.3 collective-permute-start.9
  155.1 0.0 collective-permute-done.8
  155.1 1.9 collective-permute-done.9
  157.0 0.4 maximum_convert_fusion.2.ext
  157.4 16.0 %shard_map.97 = f32[3072,64]{1,0:T(8,128)S(1)} custom-call(s32[125,128]{1,0:T(8,128)S(1)} %copy-done, f32[128]{0:T(128)S(1)} %copy-done.1, s32[1]{0:T(128)S(6)} %copy.20.live, bf16[128,128]{1,0:T(8,128)(2,1)S(1)} %pad.5.stiff, f32[3072,128]{1,0:T(8,128)S(1)} %maximum_convert_fusion.2.ext), custom_call_target="tpu_custom_call" | custom-call | tf_op jit(solution)/shard_map/pallas_call | solution.py:104
  173.5 5.4 %collective-permute-start.10 = (f32[512,64]{1,0:T(8,128)S(1)}, f32[512,64]{1,0:T(8,128)S(1)}, u32[]{:S(2)}, u32[]{:S(2)}) collective-permute-start(f32[512,64]{1,0:T(8,128)S(1)} %get-tuple-element.10), channel_id=1, source_target_pairs={{0,4},{4,8},{8,12},{12,16},{16,20},{20,24},{24,28},{1,5},{5,9},{9,... | collective-permute-start | bytes 393224 | tf_op jit(solution)/shard_map/ppermute | solution.py:134
  178.9 1.3 collective-permute-start.11
  180.2 0.3 slice_add_fusion
  180.5 0.0 collective-permute-done.10
  180.5 23.5 %collective-permute-done.11 = f32[512,64]{1,0:T(8,128)S(1)} collective-permute-done((f32[512,64]{1,0:T(8,128)S(1)}, f32[512,64]{1,0:T(8,128)S(1)}, u32[]{:S(2)}, u32[]{:S(2)}) %collective-permute-start.11) | collective-permute-done | bytes 131104 | tf_op jit(solution)/shard_map/ppermute | solution.py:135
  204.1 6.2 %scatter_custom_fusion.2 = f32[2048,64]{1,0:T(8,128)S(1)} fusion(f32[2048,64]{1,0:T(8,128)S(1)} %slice_add_fusion, s32[1024]{0:T(1024)S(1)} %bitcast.29, f32[512,64]{1,0:T(8,128)S(1)} %collective-permute-done.11, f32[]{:T(128)} %constant.24, f32[512,64]{1,0:T(8,128)S(1)} %collective-permute-done.10), kind=kCustom, calls=%fused_computation.35 | custom fusion | flops 131072 | bytes 1048580 | tf_op jit(solution)/shard_map/scatter-add | solution.py:139
  210.2 0.0 all-gather.2.cloned.1.call-done
  210.3 2.3 convolution_multiply_fusion
  212.6 0.0 reduce-scatter.2.cloned.1.call-update
  212.6 1.1 copy.16
  213.7 36.2 %reduce-scatter.2.cloned.1.call-done = f32[32,64]{1,0:T(8,128)} async-done(((f32[256,64]{1,0:T(8,128)}), f32[32,64]{1,0:T(8,128)}) %reduce-scatter.2.cloned.1.call-update) | async-done | bytes 8208 | tf_op jit(solution)/shard_map/reduce_scatter | solution.py:160
  (15 shorter events, 0.2 us)
Async XLA Ops:
  7.2 8.5 %copy-start.5 = (s32[1,2,512]{2,1,0:T(2,128)S(1)}, s32[1,2,512]{2,1,0:T(2,128)}, u32[]{:S(2)}) copy-start(s32[1,2,512]{2,1,0:T(2,128)} %param.14) | copy-start | bytes 12292
  7.2 8.5 %copy-start.4 = (f32[125,125]{1,0:T(8,128)S(1)}, f32[125,125]{1,0:T(8,128)}, u32[]{:S(2)}) copy-start(f32[125,125]{1,0:T(8,128)} %param.9) | copy-start | bytes 187504
  7.2 9.2 %copy-start.6 = (f32[2]{0:T(128)S(1)}, f32[2]{0:T(128)}, u32[]{:S(2)}) copy-start(f32[2]{0:T(128)} %param.15) | copy-start | bytes 28
  7.2 203.1 %all-gather.2.cloned.1.call-start = ((), (), s32[]{:S(2)}) async-start(), calls=%async_computation.1 | async-start | bytes 1310720 | tf_op jit(solution)/shard_map/all_gather | solution.py:152
  10.6 7.1 %collective-permute-start = (bf16[512,64]{1,0:T(8,128)(2,1)S(1)}, bf16[512,64]{1,0:T(8,128)(2,1)S(1)}, u32[]{:S(2)}, u32[]{:S(2)}) collective-permute-start(bf16[512,64]{1,0:T(8,128)(2,1)S(1)} %gather_fusion), channel_id=1, source_target_pairs={{0,4},{4,8},{8,12},{12,16},{16,20},{20,24},{24,28},{1,5},{5,9},{9,... | collective-permute-start | bytes 196616 | tf_op jit(solution)/shard_map/ppermute | solution.py:130
  13.0 7.1 %copy-start = (s32[125,128]{1,0:T(8,128)S(1)}, s32[125,128]{1,0:T(8,128)}, u32[]{:S(2)}) copy-start(s32[125,128]{1,0:T(8,128)} %connect.5) | copy-start | bytes 192004
  13.0 7.1 %copy-start.1 = (f32[128]{0:T(128)S(1)}, f32[128]{0:T(128)}, u32[]{:S(2)}) copy-start(f32[128]{0:T(128)} %scale.5) | copy-start | bytes 1540
  14.4 5.3 %collective-permute-start.1 = (bf16[512,64]{1,0:T(8,128)(2,1)S(1)}, bf16[512,64]{1,0:T(8,128)(2,1)S(1)}, u32[]{:S(2)}, u32[]{:S(2)}) collective-permute-start(bf16[512,64]{1,0:T(8,128)(2,1)S(1)} %gather_fusion.1), channel_id=1, source_target_pairs={{4,0},{8,4},{12,8},{16,12},{20,16},{24,20},{28,24},{5,1},{9,5},{13... | collective-permute-start | bytes 196616 | tf_op jit(solution)/shard_map/ppermute | solution.py:131
  20.1 22.9 %copy-start.3 = (f32[2048]{0:T(1024)S(1)}, f32[2048]{0:T(1024)}, u32[]{:S(2)}) copy-start(f32[2048]{0:T(1024)} %param.11) | copy-start | bytes 24580
  36.2 7.1 %collective-permute-start.2 = (f32[512,64]{1,0:T(8,128)S(1)}, f32[512,64]{1,0:T(8,128)S(1)}, u32[]{:S(2)}, u32[]{:S(2)}) collective-permute-start(f32[512,64]{1,0:T(8,128)S(1)} %get-tuple-element.14), channel_id=1, source_target_pairs={{0,4},{4,8},{8,12},{12,16},{16,20},{20,24},{24,28},{1,5},{5,9},{9,... | collective-permute-start | bytes 393224 | tf_op jit(solution)/shard_map/ppermute | solution.py:134
  41.7 25.6 %collective-permute-start.3 = (f32[512,64]{1,0:T(8,128)S(1)}, f32[512,64]{1,0:T(8,128)S(1)}, u32[]{:S(2)}, u32[]{:S(2)}) collective-permute-start(f32[512,64]{1,0:T(8,128)S(1)} %get-tuple-element.15), channel_id=1, source_target_pairs={{4,0},{8,4},{12,8},{16,12},{20,16},{24,20},{28,24},{5,1},{9,5},{13... | collective-permute-start | bytes 393224 | tf_op jit(solution)/shard_map/ppermute | solution.py:135
  77.0 8.7 %collective-permute-start.4 = (bf16[512,64]{1,0:T(8,128)(2,1)S(1)}, bf16[512,64]{1,0:T(8,128)(2,1)S(1)}, u32[]{:S(2)}, u32[]{:S(2)}) collective-permute-start(bf16[512,64]{1,0:T(8,128)(2,1)S(1)} %gather_fusion.2), channel_id=1, source_target_pairs={{0,4},{4,8},{8,12},{12,16},{16,20},{20,24},{24,28},{1,5},{5,9},{9,... | collective-permute-start | bytes 196616 | tf_op jit(solution)/shard_map/ppermute | solution.py:130
  83.6 3.2 %collective-permute-start.5 = (bf16[512,64]{1,0:T(8,128)(2,1)S(1)}, bf16[512,64]{1,0:T(8,128)(2,1)S(1)}, u32[]{:S(2)}, u32[]{:S(2)}) collective-permute-start(bf16[512,64]{1,0:T(8,128)(2,1)S(1)} %gather_fusion.3), channel_id=1, source_target_pairs={{4,0},{8,4},{12,8},{16,12},{20,16},{24,20},{28,24},{5,1},{9,5},{13... | collective-permute-start | bytes 196616 | tf_op jit(solution)/shard_map/ppermute | solution.py:131
  103.3 6.6 %collective-permute-start.6 = (f32[512,64]{1,0:T(8,128)S(1)}, f32[512,64]{1,0:T(8,128)S(1)}, u32[]{:S(2)}, u32[]{:S(2)}) collective-permute-start(f32[512,64]{1,0:T(8,128)S(1)} %get-tuple-element.12), channel_id=1, source_target_pairs={{0,4},{4,8},{8,12},{12,16},{16,20},{20,24},{24,28},{1,5},{5,9},{9,... | collective-permute-start | bytes 393224 | tf_op jit(solution)/shard_map/ppermute | solution.py:134
  108.3 25.6 %collective-permute-start.7 = (f32[512,64]{1,0:T(8,128)S(1)}, f32[512,64]{1,0:T(8,128)S(1)}, u32[]{:S(2)}, u32[]{:S(2)}) collective-permute-start(f32[512,64]{1,0:T(8,128)S(1)} %get-tuple-element.13), channel_id=1, source_target_pairs={{4,0},{8,4},{12,8},{16,12},{20,16},{24,20},{28,24},{5,1},{9,5},{13... | collective-permute-start | bytes 393224 | tf_op jit(solution)/shard_map/ppermute | solution.py:135
  140.3 1.0 copy-start.2
  144.4 105.5 %reduce-scatter.2.cloned.1.call-start = ((), (), s32[]{:S(2)}) async-start(), calls=%async_computation.2 | async-start | bytes 147456 | tf_op jit(solution)/shard_map/reduce_scatter | solution.py:160
  147.1 8.0 %collective-permute-start.8 = (bf16[512,64]{1,0:T(8,128)(2,1)S(1)}, bf16[512,64]{1,0:T(8,128)(2,1)S(1)}, u32[]{:S(2)}, u32[]{:S(2)}) collective-permute-start(bf16[512,64]{1,0:T(8,128)(2,1)S(1)} %gather_fusion.4), channel_id=1, source_target_pairs={{0,4},{4,8},{8,12},{12,16},{16,20},{20,24},{24,28},{1,5},{5,9},{9,... | collective-permute-start | bytes 196616 | tf_op jit(solution)/shard_map/ppermute | solution.py:130
  153.8 3.2 %collective-permute-start.9 = (bf16[512,64]{1,0:T(8,128)(2,1)S(1)}, bf16[512,64]{1,0:T(8,128)(2,1)S(1)}, u32[]{:S(2)}, u32[]{:S(2)}) collective-permute-start(bf16[512,64]{1,0:T(8,128)(2,1)S(1)} %gather_fusion.5), channel_id=1, source_target_pairs={{4,0},{8,4},{12,8},{16,12},{20,16},{24,20},{28,24},{5,1},{9,5},{13... | collective-permute-start | bytes 196616 | tf_op jit(solution)/shard_map/ppermute | solution.py:131
  173.5 7.0 %collective-permute-start.10 = (f32[512,64]{1,0:T(8,128)S(1)}, f32[512,64]{1,0:T(8,128)S(1)}, u32[]{:S(2)}, u32[]{:S(2)}) collective-permute-start(f32[512,64]{1,0:T(8,128)S(1)} %get-tuple-element.10), channel_id=1, source_target_pairs={{0,4},{4,8},{8,12},{12,16},{16,20},{20,24},{24,28},{1,5},{5,9},{9,... | collective-permute-start | bytes 393224 | tf_op jit(solution)/shard_map/ppermute | solution.py:134
  178.9 25.2 %collective-permute-start.11 = (f32[512,64]{1,0:T(8,128)S(1)}, f32[512,64]{1,0:T(8,128)S(1)}, u32[]{:S(2)}, u32[]{:S(2)}) collective-permute-start(f32[512,64]{1,0:T(8,128)S(1)} %get-tuple-element.11), channel_id=1, source_target_pairs={{4,0},{8,4},{12,8},{16,12},{20,16},{24,20},{28,24},{5,1},{9,5},{13... | collective-permute-start | bytes 393224 | tf_op jit(solution)/shard_map/ppermute | solution.py:135
Sparse Core Ops, SparseCore 0:
  144.5 31.6 all-gather.1
  212.7 37.0 reduce-scatter.1

commit v2 on v1

v2 whole, which is shorter than its diff:
```python
import functools
import math

import jax
import jax.numpy as jnp
from jax import lax
from jax.experimental import pallas as pl
from jax.experimental.pallas import tpu as pltpu
from jax.sharding import PartitionSpec as P

sigma_one = -0.5
sigma_two = 1.0 / (2.0 / sigma_one - sigma_one)

LANES = 128
HALF = LANES // 2
WAYS = 8
SHARED_WAYS = 2
MIB = 1024 * 1024
VMEM = pl.BlockSpec(memory_space=pltpu.VMEM)
SMEM = pl.BlockSpec(memory_space=pltpu.SMEM)


def low_half():
    return lax.broadcasted_iota(jnp.int32, (1, LANES), 1) < HALF


def swapped(block):
    return pltpu.roll(block, HALF, axis=1)


def chunks(rows, body):
    size = math.gcd(rows, 256)

    @pl.loop(0, rows // size)
    def _(step):
        body(pl.ds(pl.multiple_of(step * size, size), size))


def clear(refs):
    def body(at):
        for ref in refs:
            ref[at, :] = jnp.zeros((at.size, LANES), ref.dtype)

    chunks(refs[0].shape[0], body)


def sum_of(refs, at):
    total = refs[0][at, :]
    for ref in refs[1:]:
        total += ref[at, :]
    return total


def cell_kernel(
    nodes,
    capacity,
    connect,
    scale,
    live,
    stiff,
    own,
    from_low,
    from_high,
    out,
    out_low,
    out_high,
    ext,
    x0,
    x1,
    p0,
    p1,
    *sums,
):
    lows, highs = sums[:WAYS], sums[WAYS:]
    node_dev = own.shape[0]
    half = from_low.shape[0]
    low_lanes = low_half()
    clear(sums)

    def copy_own(at):
        ext[pl.ds(pl.multiple_of(at.start + 2 * half, at.size), at.size), :] = own[at, :]

    chunks(node_dev, copy_own)
    for first_row, part in ((0, from_low), (2 * half + node_dev, from_high)):
        value = part[...].astype(jnp.float32)
        other = swapped(value)
        ext[first_row : first_row + half, :] = jnp.where(low_lanes, value, other)
        ext[first_row + half : first_row + 2 * half, :] = jnp.where(low_lanes, other, value)

    live_count = live[0]
    pairs = (live_count + 1) // 2
    last = capacity // 2 - 1

    def cells_of(pair):
        first = jnp.minimum(pair, last) * 2
        return first, first + 1

    def move(scatter_pair, p, gather_pair, x):
        for begin in range(0, nodes, WAYS):
            todo = []
            for way in range(min(WAYS, nodes - begin)):
                j = begin + way
                if p is not None:
                    term = p[j : j + 1, :]
                    for sums_of, cell in zip((lows, highs), cells_of(scatter_pair)):
                        at = pl.ds(connect[j, cell], 1)
                        todo.append((sums_of[way], at, sums_of[way][at, :] + term))
                first, second = cells_of(gather_pair)
                low = ext[pl.ds(connect[j, first], 1), :]
                high = ext[pl.ds(connect[j, second], 1), :]
                todo.append((x, pl.ds(j, 1), jnp.where(low_lanes, low, high)))
            for ref, at, value in todo:
                ref[at, :] = value

    def multiply(pair, x, p):
        first, second = cells_of(pair)
        low = jnp.where(pair * 2 < live_count, scale[first], 0.0)
        high = jnp.where(pair * 2 + 1 < live_count, scale[second], 0.0)
        weight = jnp.where(low_lanes, low, high)
        p[...] = weight * jnp.dot(
            stiff[...], x[...].astype(jnp.bfloat16), preferred_element_type=jnp.float32
        )

    x0[...] = jnp.zeros_like(x0)
    x1[...] = jnp.zeros_like(x1)
    move(0, None, 0, x0)
    multiply(0, x0, p0)
    move(0, None, 1, x1)

    @pl.loop(0, (pairs + 1) // 2)
    def _(turn):
        pair = turn * 2
        multiply(pair + 1, x1, p1)
        move(pair, p0, pair + 2, x0)
        multiply(pair + 2, x0, p0)
        move(pair + 1, p1, pair + 3, x1)

    def total(at):
        both = jnp.where(low_lanes, sum_of(lows, at), sum_of(highs, at))
        return both + swapped(both)

    def write_own(at):
        out[at, :] = total(pl.ds(pl.multiple_of(at.start + 2 * half, at.size), at.size))

    chunks(node_dev, write_own)
    for first_row, part in ((0, out_low), (2 * half + node_dev, out_high)):
        part[...] = jnp.where(
            low_lanes, total(pl.ds(first_row, half)), total(pl.ds(first_row + half, half))
        )


def cell_sums(own, from_low, from_high, stiff, connect, scale, live):
    nodes, capacity = connect.shape
    depth = stiff.shape[0]
    half = from_low.shape[0]
    rows = own.shape[0] + 4 * half
    return pl.pallas_call(
        functools.partial(cell_kernel, nodes, capacity),
        out_shape=[jax.ShapeDtypeStruct(own.shape, jnp.float32)]
        + [jax.ShapeDtypeStruct((half, LANES), jnp.float32)] * 2,
        in_specs=[SMEM, SMEM, SMEM] + [VMEM] * 4,
        out_specs=[VMEM] * 3,
        scratch_shapes=[pltpu.VMEM((rows, LANES), jnp.float32)]
        + [pltpu.VMEM((depth, LANES), jnp.float32)] * 4
        + [pltpu.VMEM((rows, LANES), jnp.float32)] * (2 * WAYS),
        compiler_params=pltpu.CompilerParams(vmem_limit_bytes=48 * MIB),
    )(connect, scale, live, stiff, own, from_low, from_high)


def gather_shared(shared, half, wide, send_low, send_high):
    low_lanes = low_half()
    group = math.gcd(half, 16)

    @pl.loop(0, half // group)
    def _(turn):
        todo = []
        for k in range(group):
            j = turn * group + k
            for side, send in ((0, send_low), (1, send_high)):
                first = wide[pl.ds(shared[side, j], 1), :]
                second = wide[pl.ds(shared[side, j + half], 1), :]
                todo.append((send, pl.ds(j, 1), jnp.where(low_lanes, first, second)))
        for ref, at, value in todo:
            ref[at, :] = value


def gather_kernel(shared, wide, send_low, send_high, packed_low, packed_high):
    half = packed_low.shape[0]
    gather_shared(shared, half, wide, packed_low, packed_high)
    send_low[...] = packed_low[...].astype(send_low.dtype)
    send_high[...] = packed_high[...].astype(send_high.dtype)


def first_sends(shared, wide):
    half = shared.shape[1] // 2
    return pl.pallas_call(
        gather_kernel,
        out_shape=[jax.ShapeDtypeStruct((half, LANES), jnp.bfloat16)] * 2,
        in_specs=[SMEM, VMEM],
        out_specs=[VMEM] * 2,
        scratch_shapes=[pltpu.VMEM((half, LANES), jnp.float32)] * 2,
    )(shared, wide)


def assemble_kernel(stage, shared, window, totals, from_low, from_high, potential, before, start, *refs):
    outs = {"first": 3, "second": 4, "third": 1}[stage]
    out, scratch = refs[:outs], refs[outs:]
    sums, scratch = scratch[: 4 * SHARED_WAYS], scratch[4 * SHARED_WAYS :]
    half = from_low.shape[0]
    low_lanes = low_half()
    clear(sums)
    group = math.gcd(half, 8)

    @pl.loop(0, half // group)
    def _(turn):
        for begin in range(0, group, SHARED_WAYS):
            todo = []
            for way in range(SHARED_WAYS):
                j = turn * group + begin + way
                for side, part in ((0, from_low), (1, from_high)):
                    term = part[pl.ds(j, 1), :]
                    for upper in range(2):
                        total = sums[way * 4 + side * 2 + upper]
                        at = pl.ds(shared[side, j + upper * half], 1)
                        todo.append((total, at, total[at, :] + term))
            for ref, at, value in todo:
                ref[at, :] = value

    center = window[0]
    half_width = window[1]
    lows = [sums[k] for k in range(0, len(sums), 2)]
    highs = [sums[k] for k in range(1, len(sums), 2)]

    def pointwise(at):
        both = jnp.where(low_lanes, sum_of(lows, at), sum_of(highs, at))
        value = before[at, :]
        applied = totals[at, :] + (both + swapped(both)) + potential[at, :] * value
        if stage == "first":
            passed = (applied - center * value) * (sigma_one / half_width)
            out[0][at, :] = passed.astype(jnp.bfloat16).astype(jnp.float32)
        elif stage == "second":
            filtered = (applied - center * value) * (
                2.0 * sigma_two / half_width
            ) - sigma_one * sigma_two * start[at, :]
            out[3][at, :] = filtered
            out[0][at, :] = filtered.astype(jnp.bfloat16).astype(jnp.float32)
        else:
            out[0][at, :] = applied

    chunks(totals.shape[0], pointwise)
    if stage != "third":
        gather_shared(shared, half, out[0], scratch[0], scratch[1])
        out[1][...] = scratch[0][...].astype(out[1].dtype)
        out[2][...] = scratch[1][...].astype(out[2].dtype)


def assemble(stage, shared, window, totals, from_low, from_high, potential, before, start):
    half = from_low.shape[0]
    whole = jax.ShapeDtypeStruct(totals.shape, jnp.float32)
    packed = jax.ShapeDtypeStruct((half, LANES), jnp.bfloat16)
    out_shape = {
        "first": [whole, packed, packed],
        "second": [whole, packed, packed, whole],
        "third": [whole],
    }[stage]
    return pl.pallas_call(
        functools.partial(assemble_kernel, stage),
        out_shape=out_shape,
        in_specs=[SMEM, SMEM] + [VMEM] * 6,
        out_specs=[VMEM] * len(out_shape),
        scratch_shapes=[pltpu.VMEM(totals.shape, jnp.float32)] * (4 * SHARED_WAYS)
        + [pltpu.VMEM((half, LANES), jnp.float32)] * 2,
        compiler_params=pltpu.CompilerParams(vmem_limit_bytes=32 * MIB),
    )(shared, window, totals, from_low, from_high, potential, before, start)


def exchange_kernel(count, send_low, send_high, from_low, from_high, slot_low, slot_high, sems):
    me = lax.axis_index("cells")
    has_low = me > 0
    has_high = me < count - 1
    barrier = pltpu.get_barrier_semaphore()

    @pl.when(has_low)
    def _():
        pl.semaphore_signal(
            barrier, inc=1, device_id={"cells": me - 1}, device_id_type=pl.DeviceIdType.MESH
        )

    @pl.when(has_high)
    def _():
        pl.semaphore_signal(
            barrier, inc=1, device_id={"cells": me + 1}, device_id_type=pl.DeviceIdType.MESH
        )

    pl.semaphore_wait(barrier, jnp.minimum(me, 1) + jnp.minimum(count - 1 - me, 1))

    def copy(source, slot, place, target):
        return pltpu.make_async_remote_copy(
            src_ref=source,
            dst_ref=slot,
            send_sem=sems.at[place],
            recv_sem=sems.at[place + 1],
            device_id={"cells": target},
            device_id_type=pl.DeviceIdType.MESH,
        )

    down = copy(send_low, slot_high, 0, me - 1)
    up = copy(send_high, slot_low, 2, me + 1)

    @pl.when(has_low)
    def _():
        down.start()

    @pl.when(has_high)
    def _():
        up.start()

    @pl.when(has_low)
    def _():
        up.wait_recv()
        from_low[...] = slot_low[...]

    @pl.when(jnp.logical_not(has_low))
    def _():
        from_low[...] = jnp.zeros_like(from_low)

    @pl.when(has_high)
    def _():
        down.wait_recv()
        from_high[...] = slot_high[...]

    @pl.when(jnp.logical_not(has_high))
    def _():
        from_high[...] = jnp.zeros_like(from_high)

    @pl.when(has_low)
    def _():
        down.wait_send()

    @pl.when(has_high)
    def _():
        up.wait_send()


def exchange(send_low, send_high, collective_id):
    shape = jax.ShapeDtypeStruct(send_low.shape, send_low.dtype)
    return pl.pallas_call(
        functools.partial(exchange_kernel, lax.axis_size("cells")),
        out_shape=[shape] * 2,
        in_specs=[VMEM] * 2,
        out_specs=[VMEM] * 2,
        scratch_shapes=[pltpu.VMEM(send_low.shape, send_low.dtype)] * 2
        + [pltpu.SemaphoreType.DMA((4,))],
        compiler_params=pltpu.CompilerParams(collective_id=collective_id, has_side_effects=True),
    )(send_low, send_high)


def reduce_kernel(count, parts, out, slots, send_sems, recv_sems):
    me = lax.axis_index("cells")
    barrier = pltpu.get_barrier_semaphore()

    @pl.loop(1, count)
    def _(step):
        pl.semaphore_signal(
            barrier,
            inc=1,
            device_id={"cells": lax.rem(me + step, count)},
            device_id_type=pl.DeviceIdType.MESH,
        )

    pl.semaphore_wait(barrier, count - 1)

    def copy(step):
        target = lax.rem(me + step, count)
        return pltpu.make_async_remote_copy(
            src_ref=parts.at[target],
            dst_ref=slots.at[step],
            send_sem=send_sems.at[step],
            recv_sem=recv_sems.at[step],
            device_id={"cells": target},
            device_id_type=pl.DeviceIdType.MESH,
        )

    @pl.loop(1, count)
    def _(step):
        copy(step).start()

    out[...] = parts[me]

    @pl.loop(1, count)
    def _(step):
        copy(step).wait_recv()
        out[...] += slots[step]

    @pl.loop(1, count)
    def _(step):
        copy(step).wait_send()


def reduce_parts(parts, collective_id):
    count, rows, columns = parts.shape
    return pl.pallas_call(
        functools.partial(reduce_kernel, count),
        out_shape=jax.ShapeDtypeStruct((rows, columns), jnp.float32),
        in_specs=[VMEM],
        out_specs=VMEM,
        scratch_shapes=[
            pltpu.VMEM(parts.shape, jnp.float32),
            pltpu.SemaphoreType.DMA((count,)),
            pltpu.SemaphoreType.DMA((count,)),
        ],
        compiler_params=pltpu.CompilerParams(collective_id=collective_id, has_side_effects=True),
    )(parts)


def local(waves, stiffness, cell_scale, potential, connect, live_cells, shared, window):
    columns, node_dev = waves.shape
    assert columns == HALF
    nodes = connect.shape[0]
    depth = -(-nodes // LANES) * LANES
    stiff = jnp.pad(stiffness, ((0, depth - nodes), (0, depth - nodes))).astype(jnp.bfloat16)
    lists = shared[0]
    potential_wide = jnp.broadcast_to(potential[:, None], (node_dev, LANES))
    count = lax.axis_size("cells")

    def totals_of(own, send_low, send_high):
        from_low, from_high = exchange(send_low, send_high, 0)
        totals, to_low, to_high = cell_sums(
            own, from_low, from_high, stiff, connect, cell_scale, live_cells
        )
        return totals, *exchange(to_low, to_high, 1)

    start = jnp.concatenate([waves, waves], axis=0).T.astype(jnp.float32)
    first, *sends = assemble(
        "first",
        lists,
        window,
        *totals_of(start, *first_sends(lists, start)),
        potential_wide,
        start,
        start,
    )
    second, send_low, send_high, filtered = assemble(
        "second", lists, window, *totals_of(first, *sends), potential_wide, first, start
    )
    wave_rounded = second[:, :columns].astype(jnp.bfloat16)
    gathered = lax.all_gather(wave_rounded, "bands", axis=1, tiled=True)
    (applied,) = assemble(
        "third",
        lists,
        window,
        *totals_of(second, send_low, send_high),
        potential_wide,
        filtered,
        start,
    )
    apply_rounded = applied[:, :columns].astype(jnp.bfloat16)
    partial_value = jnp.einsum(
        "nw,nv->wv", gathered, apply_rounded, preferred_element_type=jnp.float32
    ) * (1.0 / (node_dev * count))
    projected = reduce_parts(partial_value.reshape(count, -1, columns), 2)
    return (filtered[:, :columns].T, projected)


def solution(mesh):
    return jax.shard_map(
        local,
        mesh=mesh,
        in_specs=(
            P("bands", "cells"),
            P(),
            P("cells"),
            P("cells"),
            P(None, "cells"),
            P("cells"),
            P("cells", None, None),
            P(),
        ),
        out_specs=(P("bands", "cells"), P("cells", "bands")),
        check_vma=False,
    )
```

time: 258 us -> 244 us (0.946); the launches traced: 257 us -> 240 us
  Pallas kernels: 48.1 us -> 183 us
  waiting for transfers between devices: 113 us -> 0.02 us
  starting transfers between devices: 39.3 us -> 0.04 us
  local copies, waits for them, and re-layouts: 13 us -> 37.9 us
  other arithmetic: 24.6 us -> 2.11 us
    pallas_call x3 -> x14, Pallas kernels: 48.1 us -> 183 us  [the longest x6 112 us: exchange(): pl.pallas_call(functools.partial(exchange_kernel, lax.axis_size('cells'))...]
    ppermute x12 -> x0, waiting for transfers between devices: 76.6 us -> none  [the longest x3 71.4 us: apply(): from_upper = lax.ppermute(totals[:ghost], 'cells', backward)]
    ppermute x12 -> x0, starting transfers between devices: 39.3 us -> none  [the longest x3 15.8 us: apply(): from_lower = lax.ppermute(totals[ghost + node_dev:], 'cells', forward)]
    reduce_scatter x1 -> x0, waiting for transfers between devices: 36.2 us -> none  [local(): lax.psum_scatter(partial_value, 'cells', scatter_dimension=0, tiled=True)]
    unnamed x16 -> x81, local copies, waits for them, and re-layouts: 3.35 us -> 33 us
    scatter-add x3 -> x0, other arithmetic: 18.7 us -> none  [apply(): return totals[ghost:ghost + node_dev].at[jnp.concatenate([low_nodes, high...]
    gather x6 -> x0, local copies, waits for them, and re-layouts: 8.05 us -> none  [the longest x3 4.03 us: apply(): upper = lax.ppermute(owned[low_nodes], 'cells', backward)]
    convert_element_type x5 -> x1, other arithmetic: 4.14 us -> 1.26 us  [local(): start = jnp.concatenate([waves, waves], axis=0).T.astype(jnp.float32)]
  transfers between devices with their start and end apart: 14 -> 1, of which waited for: 7 -> 0; matrix products, arithmetic and copies ran while one was open for 5% -> 1% of each run, Pallas kernels for 6% -> 23%
where the time goes in v2:
time: 244 us; the launch traced here: 240 us
  Pallas kernels  183 us (75%)
  local copies, waits for them, and re-layouts  37.9 us (16%)
  between operations  14.9 us (6%)
    pallas_call x6, Pallas kernels, exchange(): pl.pallas_call(functools.partial(exchange_kernel, lax.axis_size('cells'))...  112 us
    pallas_call x3, Pallas kernels, cell_sums(): pl.pallas_call(functools.partial(cell_kernel, nodes, capacity), out_shape...  43 us
    unnamed x81, local copies, waits for them, and re-layouts  33 us
    pallas_call x3, Pallas kernels, assemble(): pl.pallas_call(functools.partial(assemble_kernel, stage), out_shape=out_s...  14.7 us
    pallas_call x1, Pallas kernels, reduce_parts(): pl.pallas_call(functools.partial(reduce_kernel, count), out_shape=jax.Sha...  9.88 us
  transfers between devices with their start and end apart: 1, of which 0 were waited for; matrix products, arithmetic and copies ran while one was open for 1% of the time, Pallas kernels for 23%

profile of v2, /device:TPU:0, one launch (start us, length us, event | category | flops | bytes accessed | tf_op | source)
XLA Modules:
  0.0 240.1 jit_solution(9477248677754974710)
XLA Ops:
  7.2 0.0 all-gather.2.cloned.1.call-start
  7.9 0.8 convert.11
  8.7 1.2 copy.14
  9.9 1.3 convert_bitcast_fusion.wide.own.before.start
  11.2 3.5 %shard_map.95 = (bf16[256,128]{1,0:T(8,128)(2,1)}, bf16[256,128]{1,0:T(8,128)(2,1)}) custom-call(s32[2,512]{1,0:T(2,128)} %bitcast.7, f32[2048,128]{1,0:T(8,128)} %convert_bitcast_fusion.wide.own.before.start), custom_call_target="tpu_custom_call" | custom-call | tf_op jit(solution)/shard_map/pallas_call | solution.py:196
  14.8 5.4 %shard_map.96 = (bf16[256,128]{1,0:T(8,128)(2,1)}, bf16[256,128]{1,0:T(8,128)(2,1)}) custom-call(bf16[256,128]{1,0:T(8,128)(2,1)} %get-tuple-element.32.send_low, bf16[256,128]{1,0:T(8,128)(2,1)} %get-tuple-element.33.send_high), custom_call_target="tpu_custom_call" | custom-call | tf_op jit(solution)/shard_map/pallas_call | solution.py:347
  20.2 0.0 copy-start.36
  20.2 0.6 copy-done.36
  20.8 0.8 copy-done.29
  21.7 0.8 copy-done.30
  22.5 14.3 %shard_map.97 = (f32[2048,128]{1,0:T(8,128)S(1)}, f32[256,128]{1,0:T(8,128)S(1)}, f32[256,128]{1,0:T(8,128)S(1)}) custom-call(s32[125,128]{1,0:T(8,128)S(1)} %copy-done.12, f32[128]{0:T(128)S(1)} %copy-done.36, s32[1]{0:T(128)S(6)} %copy.20.live, bf16[128,128]{1,0:T(8,128)(2,1)S(1)} %pad.5.stiff, f32[2048,128]{1,0:T(8,128)S(1)} %copy-done, ...), custom_call_target="tpu_custom_call" | custom-call | tf_op jit(solution)/shard_map/pallas_call | solution.py:157
  36.8 1.0 copy-done.10
  37.8 0.7 copy-done.21
  38.5 0.6 copy-done.22
  39.1 31.6 %shard_map.98 = (f32[256,128]{1,0:T(8,128)}, f32[256,128]{1,0:T(8,128)}) custom-call(f32[256,128]{1,0:T(8,128)} %copy-done.21, f32[256,128]{1,0:T(8,128)} %copy-done.22), custom_call_target="tpu_custom_call" | custom-call | tf_op jit(solution)/shard_map/pallas_call | solution.py:347
  70.7 0.3 broadcast_in_dim.2.potential
  71.1 0.0 copy-start.35
  71.1 0.0 copy-start.37
  71.1 0.9 copy-done.11
  72.0 0.9 copy-done.15
  72.9 0.9 copy-done.16
  73.8 5.5 %shard_map.99 = (f32[2048,128]{1,0:T(8,128)S(1)}, bf16[256,128]{1,0:T(8,128)(2,1)S(1)}, bf16[256,128]{1,0:T(8,128)(2,1)S(1)}) custom-call(s32[2,512]{1,0:T(2,128)S(1)} %bitcast.8, f32[2]{0:T(128)S(1)} %copy-done.37, f32[2048,128]{1,0:T(8,128)S(1)} %copy-done.11, f32[256,128]{1,0:T(8,128)S(1)} %copy-done.15, f32[256,128]{1,0:T(8,128)S(1)} %copy-done.16, ...), custom_call_target="tpu_custom_call" | custom-call | tf_op jit(solution)/shard_map/pallas_call | solution.py:266
  79.2 0.0 copy-start.33
  79.2 0.6 copy-done.33
  79.9 0.6 copy-done.34
  80.5 6.0 %shard_map.100 = (bf16[256,128]{1,0:T(8,128)(2,1)}, bf16[256,128]{1,0:T(8,128)(2,1)}) custom-call(bf16[256,128]{1,0:T(8,128)(2,1)} %copy-done.33, bf16[256,128]{1,0:T(8,128)(2,1)} %copy-done.34), custom_call_target="tpu_custom_call" | custom-call | tf_op jit(solution)/shard_map/pallas_call | solution.py:347
  86.5 0.8 copy-done.27
  87.3 0.8 copy-done.28
  88.1 14.3 %shard_map.101 = (f32[2048,128]{1,0:T(8,128)S(1)}, f32[256,128]{1,0:T(8,128)S(1)}, f32[256,128]{1,0:T(8,128)S(1)}) custom-call(s32[125,128]{1,0:T(8,128)S(1)} %copy-done.12, f32[128]{0:T(128)S(1)} %copy-done.36, s32[1]{0:T(128)S(6)} %copy.20.live, bf16[128,128]{1,0:T(8,128)(2,1)S(1)} %pad.5.stiff, f32[2048,128]{1,0:T(8,128)S(1)} %get-tuple-element.41.own.before, ...), custom_call_target="tpu_custom_call" | custom-call | tf_op jit(solution)/shard_map/pallas_call | solution.py:157
  102.5 1.0 copy-done.8
  103.5 0.7 copy-done.23
  104.1 0.6 copy-done.24
  104.8 31.6 %shard_map.102 = (f32[256,128]{1,0:T(8,128)}, f32[256,128]{1,0:T(8,128)}) custom-call(f32[256,128]{1,0:T(8,128)} %copy-done.23, f32[256,128]{1,0:T(8,128)} %copy-done.24), custom_call_target="tpu_custom_call" | custom-call | tf_op jit(solution)/shard_map/pallas_call | solution.py:347
  136.4 1.2 copy-done.3
  137.6 1.2 copy-done.9
  138.8 0.9 copy-done.13
  139.7 0.9 copy-done.14
  140.6 5.5 %shard_map.103 = (f32[2048,128]{1,0:T(8,128)S(1)}, bf16[256,128]{1,0:T(8,128)(2,1)S(1)}, bf16[256,128]{1,0:T(8,128)(2,1)S(1)}, f32[2048,128]{1,0:T(8,128)S(1)}) custom-call(s32[2,512]{1,0:T(2,128)S(1)} %bitcast.9, f32[2]{0:T(128)S(1)} %copy-done.37, f32[2048,128]{1,0:T(8,128)S(1)} %copy-done.9, f32[256,128]{1,0:T(8,128)S(1)} %copy-done.13, ...), custom_call_target="tpu_custom_call" | custom-call | tf_op jit(solution)/shard_map/pallas_call | solution.py:266
  146.1 0.6 copy-done.31
  146.7 0.6 copy-done.32
  147.3 0.8 slice.20
  148.2 1.0 copy-done.4
  149.2 1.9 copy.16
  151.1 0.0 all-gather.2.cloned.1.call-update
  151.1 1.0 slice_bitcast_fusion
  152.1 2.3 copy.18
  154.5 5.9 %shard_map.104 = (bf16[256,128]{1,0:T(8,128)(2,1)}, bf16[256,128]{1,0:T(8,128)(2,1)}) custom-call(bf16[256,128]{1,0:T(8,128)(2,1)} %copy-done.31, bf16[256,128]{1,0:T(8,128)(2,1)} %copy-done.32), custom_call_target="tpu_custom_call" | custom-call | tf_op jit(solution)/shard_map/pallas_call | solution.py:347
  160.4 1.2 copy-done.5
  161.6 0.8 copy-done.25
  162.5 0.8 copy-done.26
  163.3 14.3 %shard_map.105 = (f32[2048,128]{1,0:T(8,128)S(1)}, f32[256,128]{1,0:T(8,128)S(1)}, f32[256,128]{1,0:T(8,128)S(1)}) custom-call(s32[125,128]{1,0:T(8,128)S(1)} %copy-done.12, f32[128]{0:T(128)S(1)} %copy-done.36, s32[1]{0:T(128)S(6)} %copy.20.live, bf16[128,128]{1,0:T(8,128)(2,1)S(1)} %pad.5.stiff, f32[2048,128]{1,0:T(8,128)S(1)} %copy-done.5, ...), custom_call_target="tpu_custom_call" | custom-call | tf_op jit(solution)/shard_map/pallas_call | solution.py:157
  177.6 1.0 copy-done.6
  178.6 0.6 copy-done.19
  179.3 0.6 copy-done.20
  179.9 31.6 %shard_map.106 = (f32[256,128]{1,0:T(8,128)}, f32[256,128]{1,0:T(8,128)}) custom-call(f32[256,128]{1,0:T(8,128)} %copy-done.19, f32[256,128]{1,0:T(8,128)} %copy-done.20), custom_call_target="tpu_custom_call" | custom-call | tf_op jit(solution)/shard_map/pallas_call | solution.py:347
  211.5 1.2 copy-done.7
  212.7 0.9 copy-done.17
  213.6 0.9 copy-done.18
  214.5 3.8 %shard_map.107 = f32[2048,128]{1,0:T(8,128)S(1)} custom-call(s32[2,512]{1,0:T(2,128)S(1)} %bitcast.10, f32[2]{0:T(128)S(1)} %copy-done.37, f32[2048,128]{1,0:T(8,128)S(1)} %copy-done.7, f32[256,128]{1,0:T(8,128)S(1)} %copy-done.17, f32[256,128]{1,0:T(8,128)S(1)} %copy-done.18, f32[2048,128]{1,0:T(8,128)S(1)} %broadcast_in_dim.2.potential, ...), custom_call_target="tpu_custom_call" | custom-call | tf_op jit(solution)/shard_map/pallas_call | solution.py:266
  218.3 1.0 copy-done.1
  219.3 2.0 convolution_multiply_fusion
  221.3 0.8 copy.17
  222.0 9.9 %shard_map.108 = f32[32,64]{1,0:T(8,128)} custom-call(f32[8,32,64]{2,1,0:T(8,128)} %bitcast.11), custom_call_target="tpu_custom_call" | custom-call | tf_op jit(solution)/shard_map/pallas_call | solution.py:402
  231.9 1.3 copy.21
  (43 shorter events, 0.1 us)
Async XLA Ops:
  7.2 212.1 %all-gather.2.cloned.1.call-start = ((), (), s32[]{:S(2)}) async-start(), calls=%async_computation | async-start | bytes 1310720 | tf_op jit(solution)/shard_map/all_gather | solution.py:447
  11.2 9.0 %copy-start = (f32[2048,128]{1,0:T(8,128)S(1)}, f32[2048,128]{1,0:T(8,128)}, u32[]{:S(2)}) copy-start(f32[2048,128]{1,0:T(8,128)} %convert_bitcast_fusion.wide.own.before.start) | copy-start | bytes 3145732
  14.8 5.4 %copy-start.12 = (s32[125,128]{1,0:T(8,128)S(1)}, s32[125,128]{1,0:T(8,128)}, u32[]{:S(2)}) copy-start(s32[125,128]{1,0:T(8,128)} %connect.5) | copy-start | bytes 192004
  20.2 0.7 copy-start.36
  20.8 0.8 copy-start.29
  21.7 0.8 copy-start.30
  36.8 1.0 copy-start.10
  37.8 0.7 copy-start.21
  38.5 0.7 copy-start.22
  39.1 31.6 %copy-start.38 = (f32[2048]{0:T(1024)S(1)}, f32[2048]{0:T(1024)}, u32[]{:S(2)}) copy-start(f32[2048]{0:T(1024)} %param.11) | copy-start | bytes 24580
  70.7 1.2 copy-start.11
  71.1 0.9 copy-start.35
  71.1 0.9 copy-start.37
  72.0 0.9 copy-start.15
  72.9 0.9 copy-start.16
  79.2 0.6 copy-start.33
  79.9 0.6 copy-start.34
  80.5 55.9 %copy-start.2 = (f32[2048,128]{1,0:T(8,128)}, f32[2048,128]{1,0:T(8,128)S(1)}, u32[]{:S(2)}) copy-start(f32[2048,128]{1,0:T(8,128)S(1)} %get-tuple-element.41.own.before) | copy-start | bytes 3145732
  86.5 0.8 copy-start.27
  87.3 0.8 copy-start.28
  102.5 1.0 copy-start.8
  103.5 0.7 copy-start.23
  104.1 0.7 copy-start.24
  136.4 1.2 copy-start.3
  137.6 1.2 copy-start.9
  138.8 0.9 copy-start.13
  139.7 0.9 copy-start.14
  146.1 0.6 copy-start.31
  146.7 0.6 copy-start.32
  148.2 1.0 copy-start.4
  160.4 1.3 copy-start.5
  161.6 0.8 copy-start.25
  162.5 0.8 copy-start.26
  177.6 1.0 copy-start.6
  178.6 0.7 copy-start.19
  179.3 0.6 copy-start.20
  211.5 1.2 copy-start.7
  212.7 0.9 copy-start.17
  213.6 0.9 copy-start.18
  218.3 1.0 copy-start.1
Sparse Core Ops, SparseCore 0:
  151.2 31.2 all-gather.1

commit v3 on v2

--- a/solution.py
+++ b/solution.py
@@ -13,7 +13,7 @@
 
 LANES = 128
 HALF = LANES // 2
-WAYS = 8
+WAYS = 4
 SHARED_WAYS = 2
 MIB = 1024 * 1024
 VMEM = pl.BlockSpec(memory_space=pltpu.VMEM)
@@ -58,13 +58,10 @@
     scale,
     live,
     stiff,
-    own,
-    from_low,
-    from_high,
+    ext,
     out,
     out_low,
     out_high,
-    ext,
     x0,
     x1,
     p0,
@@ -72,20 +69,10 @@
     *sums,
 ):
     lows, highs = sums[:WAYS], sums[WAYS:]
-    node_dev = own.shape[0]
-    half = from_low.shape[0]
+    node_dev = out.shape[0]
+    half = out_low.shape[0]
     low_lanes = low_half()
     clear(sums)
-
-    def copy_own(at):
-        ext[pl.ds(pl.multiple_of(at.start + 2 * half, at.size), at.size), :] = own[at, :]
-
-    chunks(node_dev, copy_own)
-    for first_row, part in ((0, from_low), (2 * half + node_dev, from_high)):
-        value = part[...].astype(jnp.float32)
-        other = swapped(value)
-        ext[first_row : first_row + half, :] = jnp.where(low_lanes, value, other)
-        ext[first_row + half : first_row + 2 * half, :] = jnp.where(low_lanes, other, value)
 
     live_count = live[0]
     pairs = (live_count + 1) // 2
@@ -106,8 +93,8 @@
                         at = pl.ds(connect[j, cell], 1)
                         todo.append((sums_of[way], at, sums_of[way][at, :] + term))
                 first, second = cells_of(gather_pair)
-                low = ext[pl.ds(connect[j, first], 1), :]
-                high = ext[pl.ds(connect[j, second], 1), :]
+                low = ext[connect[j, first]]
+                high = ext[connect[j, second]]
                 todo.append((x, pl.ds(j, 1), jnp.where(low_lanes, low, high)))
             for ref, at, value in todo:
                 ref[at, :] = value
@@ -149,22 +136,21 @@
         )
 
 
-def cell_sums(own, from_low, from_high, stiff, connect, scale, live):
+def cell_sums(ext, node_dev, stiff, connect, scale, live):
     nodes, capacity = connect.shape
     depth = stiff.shape[0]
-    half = from_low.shape[0]
-    rows = own.shape[0] + 4 * half
+    rows = ext.shape[0]
+    half = (rows - node_dev) // 4
     return pl.pallas_call(
         functools.partial(cell_kernel, nodes, capacity),
-        out_shape=[jax.ShapeDtypeStruct(own.shape, jnp.float32)]
+        out_shape=[jax.ShapeDtypeStruct((node_dev, LANES), jnp.float32)]
         + [jax.ShapeDtypeStruct((half, LANES), jnp.float32)] * 2,
-        in_specs=[SMEM, SMEM, SMEM] + [VMEM] * 4,
+        in_specs=[SMEM, SMEM, SMEM] + [VMEM] * 2,
         out_specs=[VMEM] * 3,
-        scratch_shapes=[pltpu.VMEM((rows, LANES), jnp.float32)]
-        + [pltpu.VMEM((depth, LANES), jnp.float32)] * 4
+        scratch_shapes=[pltpu.VMEM((depth, LANES), jnp.float32)] * 4
         + [pltpu.VMEM((rows, LANES), jnp.float32)] * (2 * WAYS),
-        compiler_params=pltpu.CompilerParams(vmem_limit_bytes=48 * MIB),
-    )(connect, scale, live, stiff, own, from_low, from_high)
+        compiler_params=pltpu.CompilerParams(vmem_limit_bytes=24 * MIB),
+    )(connect, scale, live, stiff, ext.reshape(rows, 1, LANES))
 
 
 def gather_shared(shared, half, wide, send_low, send_high):
@@ -199,6 +185,7 @@
         in_specs=[SMEM, VMEM],
         out_specs=[VMEM] * 2,
         scratch_shapes=[pltpu.VMEM((half, LANES), jnp.float32)] * 2,
+        compiler_params=pltpu.CompilerParams(vmem_limit_bytes=8 * MIB),
     )(shared, wide)
 
 
@@ -270,11 +257,11 @@
         out_specs=[VMEM] * len(out_shape),
         scratch_shapes=[pltpu.VMEM(totals.shape, jnp.float32)] * (4 * SHARED_WAYS)
         + [pltpu.VMEM((half, LANES), jnp.float32)] * 2,
-        compiler_params=pltpu.CompilerParams(vmem_limit_bytes=32 * MIB),
+        compiler_params=pltpu.CompilerParams(vmem_limit_bytes=20 * MIB),
     )(shared, window, totals, from_low, from_high, potential, before, start)
 
 
-def exchange_kernel(count, send_low, send_high, from_low, from_high, slot_low, slot_high, sems):
+def exchange(count, send_low, send_high, slot_low, slot_high, sems, meanwhile):
     me = lax.axis_index("cells")
     has_low = me > 0
     has_high = me < count - 1
@@ -315,23 +302,23 @@
     def _():
         up.start()
 
+    meanwhile()
+
     @pl.when(has_low)
     def _():
         up.wait_recv()
-        from_low[...] = slot_low[...]
 
     @pl.when(jnp.logical_not(has_low))
     def _():
-        from_low[...] = jnp.zeros_like(from_low)
+        slot_low[...] = jnp.zeros_like(slot_low)
 
     @pl.when(has_high)
     def _():
         down.wait_recv()
-        from_high[...] = slot_high[...]
 
     @pl.when(jnp.logical_not(has_high))
     def _():
-        from_high[...] = jnp.zeros_like(from_high)
+        slot_high[...] = jnp.zeros_like(slot_high)
 
     @pl.when(has_low)
     def _():
@@ -342,17 +329,59 @@
         up.wait_send()
 
 
-def exchange(send_low, send_high, collective_id):
+def extend_kernel(count, own, send_low, send_high, ext, slot_low, slot_high, sems):
+    node_dev = own.shape[0]
+    half = send_low.shape[0]
+    low_lanes = low_half()
+
+    def copy_own(at):
+        ext[pl.ds(pl.multiple_of(at.start + 2 * half, at.size), at.size), :] = own[at, :]
+
+    exchange(
+        count,
+        send_low,
+        send_high,
+        slot_low,
+        slot_high,
+        sems,
+        lambda: chunks(node_dev, copy_own),
+    )
+    for first_row, part in ((0, slot_low), (2 * half + node_dev, slot_high)):
+        value = part[...].astype(jnp.float32)
+        other = swapped(value)
+        ext[first_row : first_row + half, :] = jnp.where(low_lanes, value, other)
+        ext[first_row + half : first_row + 2 * half, :] = jnp.where(low_lanes, other, value)
+
+
+def swap_kernel(count, send_low, send_high, from_low, from_high, slot_low, slot_high, sems):
+    exchange(count, send_low, send_high, slot_low, slot_high, sems, lambda: None)
+    from_low[...] = slot_low[...]
+    from_high[...] = slot_high[...]
+
+
+def exchange_call(kernel, collective_id, out_shape, like, *operands):
+    return pl.pallas_call(
+        functools.partial(kernel, lax.axis_size("cells")),
+        out_shape=out_shape,
+        in_specs=[VMEM] * len(operands),
+        out_specs=[VMEM] * len(out_shape),
+        scratch_shapes=[pltpu.VMEM(like.shape, like.dtype)] * 2
+        + [pltpu.SemaphoreType.DMA((4,))],
+        compiler_params=pltpu.CompilerParams(
+            collective_id=collective_id, has_side_effects=True, vmem_limit_bytes=8 * MIB
+        ),
+    )(*operands)
+
+
+def extend(own, send_low, send_high):
+    rows = own.shape[0] + 4 * send_low.shape[0]
+    shape = jax.ShapeDtypeStruct((rows, LANES), jnp.float32)
+    return exchange_call(extend_kernel, 0, [shape], send_low, own, send_low, send_high)[0]
+
+
+def swap(send_low, send_high):
     shape = jax.ShapeDtypeStruct(send_low.shape, send_low.dtype)
-    return pl.pallas_call(
-        functools.partial(exchange_kernel, lax.axis_size("cells")),
-        out_shape=[shape] * 2,
-        in_specs=[VMEM] * 2,
-        out_specs=[VMEM] * 2,
-        scratch_shapes=[pltpu.VMEM(send_low.shape, send_low.dtype)] * 2
-        + [pltpu.SemaphoreType.DMA((4,))],
-        compiler_params=pltpu.CompilerParams(collective_id=collective_id, has_side_effects=True),
-    )(send_low, send_high)
+    return exchange_call(swap_kernel, 1, [shape] * 2, send_low, send_low, send_high)
 
 
 def reduce_kernel(count, parts, out, slots, send_sems, recv_sems):
@@ -409,7 +438,9 @@
             pltpu.SemaphoreType.DMA((count,)),
             pltpu.SemaphoreType.DMA((count,)),
         ],
-        compiler_params=pltpu.CompilerParams(collective_id=collective_id, has_side_effects=True),
+        compiler_params=pltpu.CompilerParams(
+            collective_id=collective_id, has_side_effects=True, vmem_limit_bytes=8 * MIB
+        ),
     )(parts)
 
 
@@ -424,11 +455,10 @@
     count = lax.axis_size("cells")
 
     def totals_of(own, send_low, send_high):
-        from_low, from_high = exchange(send_low, send_high, 0)
         totals, to_low, to_high = cell_sums(
-            own, from_low, from_high, stiff, connect, cell_scale, live_cells
-        )
-        return totals, *exchange(to_low, to_high, 1)
+            extend(own, send_low, send_high), node_dev, stiff, connect, cell_scale, live_cells
+        )
+        return totals, *swap(to_low, to_high)
 
     start = jnp.concatenate([waves, waves], axis=0).T.astype(jnp.float32)
     first, *sends = assemble(

time: 244 us -> 200 us (0.82)
  local copies, waits for them, and re-layouts: 37.9 us -> 13.8 us
  Pallas kernels: 183 us -> 160 us
  waiting for transfers between devices: 0.02 us -> 5.26 us
    pallas_call x6, Pallas kernels: 112 us -> 77.2 us  [exchange_call(): pl.pallas_call(functools.partial(kernel, lax.axis_size('cells')), out_sha...]
    pallas_call x1, Pallas kernels: 9.88 us -> 34.8 us  [reduce_parts(): pl.pallas_call(functools.partial(reduce_kernel, count), out_shape=jax.Sha...]
    unnamed x81 -> x23, local copies, waits for them, and re-layouts: 33 us -> 9.54 us
    pallas_call x3, Pallas kernels: 43 us -> 31.6 us  [cell_sums(): pl.pallas_call(functools.partial(cell_kernel, nodes, capacity), out_shape...]
    all_gather x1, waiting for transfers between devices: 0.01 us -> 5.25 us  [local(): gathered = lax.all_gather(wave_rounded, 'bands', axis=1, tiled=True)]
  transfers between devices with their start and end apart: 1 -> 1, of which waited for: 0 -> 1; matrix products, arithmetic and copies ran while one was open for 1% -> 2% of each run, Pallas kernels for 23% -> 26%
where the time goes in v3:
time: 200 us; the launch traced here: 198 us
  Pallas kernels  160 us (80%)
  between operations  14.9 us (7%)
  local copies, waits for them, and re-layouts  13.8 us (7%)
  waiting for transfers between devices  5.26 us (3%)
    pallas_call x6, Pallas kernels, exchange_call(): pl.pallas_call(functools.partial(kernel, lax.axis_size('cells')), out_sha...  77.2 us
    pallas_call x1, Pallas kernels, reduce_parts(): pl.pallas_call(functools.partial(reduce_kernel, count), out_shape=jax.Sha...  34.8 us
    pallas_call x3, Pallas kernels, cell_sums(): pl.pallas_call(functools.partial(cell_kernel, nodes, capacity), out_shape...  31.6 us
    pallas_call x3, Pallas kernels, assemble(): pl.pallas_call(functools.partial(assemble_kernel, stage), out_shape=out_s...  14.7 us
    unnamed x23, local copies, waits for them, and re-layouts  9.54 us
    all_gather x1, waiting for transfers between devices, local(): gathered = lax.all_gather(wave_rounded, 'bands', axis=1, tiled=True)  5.25 us
  transfers between devices with their start and end apart: 1, of which 1 were waited for; matrix products, arithmetic and copies ran while one was open for 2% of the time, Pallas kernels for 26%

profile of v3, /device:TPU:0, one launch (start us, length us, event | category | flops | bytes accessed | tf_op | source)
XLA Modules:
  0.0 197.6 jit_solution(10728877522209752928)
XLA Ops:
  7.2 0.0 copy-start.6
  7.2 0.0 all-gather.2.cloned.1.call-start
  7.9 0.8 convert.11
  8.7 1.2 copy.14
  9.9 0.3 convert_bitcast_fusion.wide.own.before.start
  10.2 0.0 copy-done.6
  10.2 2.2 %shard_map.95 = (bf16[256,128]{1,0:T(8,128)(2,1)S(1)}, bf16[256,128]{1,0:T(8,128)(2,1)S(1)}) custom-call(s32[2,512]{1,0:T(2,128)S(1)} %bitcast.14, f32[2048,128]{1,0:T(8,128)S(1)} %convert_bitcast_fusion.wide.own.before.start), custom_call_target="tpu_custom_call" | custom-call | tf_op jit(solution)/shard_map/pallas_call | solution.py:182
  12.4 0.0 copy-start.5
  12.4 0.0 copy-start.7
  12.4 4.0 %shard_map.96 = f32[3072,128]{1,0:T(8,128)S(1)} custom-call(f32[2048,128]{1,0:T(8,128)S(1)} %convert_bitcast_fusion.wide.own.before.start, bf16[256,128]{1,0:T(8,128)(2,1)S(1)} %get-tuple-element.26.send_low, bf16[256,128]{1,0:T(8,128)(2,1)S(1)} %get-tuple-element.27.send_high), custom_call_target="tpu_custom_call" | custom-call | tf_op jit(solution)/shard_map/pallas_call | solution.py:363
  16.4 0.0 copy-start.9
  16.4 0.0 copy-start.8
  16.5 0.0 copy-done.5
  16.5 0.0 copy-done.7
  16.5 10.5 %shard_map.97 = (f32[2048,128]{1,0:T(8,128)S(1)}, f32[256,128]{1,0:T(8,128)S(1)}, f32[256,128]{1,0:T(8,128)S(1)}) custom-call(s32[125,128]{1,0:T(8,128)S(1)} %copy-done.5, f32[128]{0:T(128)S(1)} %copy-done.7, s32[1]{0:T(128)S(6)} %copy.20.live, bf16[128,128]{1,0:T(8,128)(2,1)S(1)} %pad.5.stiff, f32[3072,1,128]{2,1,0:T(1,128)S(1)} %bitcast.11), custom_call_target="tpu_custom_call" | custom-call | tf_op jit(solution)/shard_map/pallas_call | solution.py:144
  27.0 5.6 %shard_map.98 = (f32[256,128]{1,0:T(8,128)S(1)}, f32[256,128]{1,0:T(8,128)S(1)}) custom-call(f32[256,128]{1,0:T(8,128)S(1)} %get-tuple-element.29.send_low, f32[256,128]{1,0:T(8,128)S(1)} %get-tuple-element.30.send_high), custom_call_target="tpu_custom_call" | custom-call | tf_op jit(solution)/shard_map/pallas_call | solution.py:363
  32.6 0.0 copy-done.9
  32.6 0.3 broadcast_in_dim.2.potential
  32.9 0.0 copy-done.8
  32.9 5.5 %shard_map.99 = (f32[2048,128]{1,0:T(8,128)S(1)}, bf16[256,128]{1,0:T(8,128)(2,1)S(1)}, bf16[256,128]{1,0:T(8,128)(2,1)S(1)}) custom-call(s32[2,512]{1,0:T(2,128)S(1)} %bitcast.15, f32[2]{0:T(128)S(1)} %copy-done.8, f32[2048,128]{1,0:T(8,128)S(1)} %get-tuple-element.28.totals, f32[256,128]{1,0:T(8,128)S(1)} %get-tuple-element.31.from_low, ...), custom_call_target="tpu_custom_call" | custom-call | tf_op jit(solution)/shard_map/pallas_call | solution.py:253
  38.4 13.5 %shard_map.100 = f32[3072,128]{1,0:T(8,128)S(1)} custom-call(f32[2048,128]{1,0:T(8,128)S(1)} %get-tuple-element.33.own.before, bf16[256,128]{1,0:T(8,128)(2,1)S(1)} %get-tuple-element.34.send_low, bf16[256,128]{1,0:T(8,128)(2,1)S(1)} %get-tuple-element.35.send_high), custom_call_target="tpu_custom_call" | custom-call | tf_op jit(solution)/shard_map/pallas_call | solution.py:363
  51.9 10.5 %shard_map.101 = (f32[2048,128]{1,0:T(8,128)S(1)}, f32[256,128]{1,0:T(8,128)S(1)}, f32[256,128]{1,0:T(8,128)S(1)}) custom-call(s32[125,128]{1,0:T(8,128)S(1)} %copy-done.5, f32[128]{0:T(128)S(1)} %copy-done.7, s32[1]{0:T(128)S(6)} %copy.20.live, bf16[128,128]{1,0:T(8,128)(2,1)S(1)} %pad.5.stiff, f32[3072,1,128]{2,1,0:T(1,128)S(1)} %bitcast.12), custom_call_target="tpu_custom_call" | custom-call | tf_op jit(solution)/shard_map/pallas_call | solution.py:144
  62.4 17.7 %shard_map.102 = (f32[256,128]{1,0:T(8,128)S(1)}, f32[256,128]{1,0:T(8,128)S(1)}) custom-call(f32[256,128]{1,0:T(8,128)S(1)} %get-tuple-element.37.send_low, f32[256,128]{1,0:T(8,128)S(1)} %get-tuple-element.38.send_high), custom_call_target="tpu_custom_call" | custom-call | tf_op jit(solution)/shard_map/pallas_call | solution.py:363
  80.1 5.5 %shard_map.103 = (f32[2048,128]{1,0:T(8,128)S(1)}, bf16[256,128]{1,0:T(8,128)(2,1)S(1)}, bf16[256,128]{1,0:T(8,128)(2,1)S(1)}, f32[2048,128]{1,0:T(8,128)S(1)}) custom-call(s32[2,512]{1,0:T(2,128)S(1)} %bitcast.16, f32[2]{0:T(128)S(1)} %copy-done.8, f32[2048,128]{1,0:T(8,128)S(1)} %get-tuple-element.36.totals, f32[256,128]{1,0:T(8,128)S(1)} %get-tuple-element.39.from_low, ...), custom_call_target="tpu_custom_call" | custom-call | tf_op jit(solution)/shard_map/pallas_call | solution.py:253
  85.6 0.8 slice.20
  86.5 0.0 copy-start.1
  86.5 1.0 copy-done.1
  87.4 1.9 copy.16
  89.4 0.0 all-gather.2.cloned.1.call-update
  89.4 0.0 copy-start.2
  89.4 1.2 copy-done.2
  90.6 18.0 %shard_map.104 = f32[3072,128]{1,0:T(8,128)S(1)} custom-call(f32[2048,128]{1,0:T(8,128)S(1)} %copy-done.2, bf16[256,128]{1,0:T(8,128)(2,1)S(1)} %get-tuple-element.43.send_low, bf16[256,128]{1,0:T(8,128)(2,1)S(1)} %get-tuple-element.44.send_high), custom_call_target="tpu_custom_call" | custom-call | tf_op jit(solution)/shard_map/pallas_call | solution.py:363
  108.6 10.5 %shard_map.105 = (f32[2048,128]{1,0:T(8,128)S(1)}, f32[256,128]{1,0:T(8,128)S(1)}, f32[256,128]{1,0:T(8,128)S(1)}) custom-call(s32[125,128]{1,0:T(8,128)S(1)} %copy-done.5, f32[128]{0:T(128)S(1)} %copy-done.7, s32[1]{0:T(128)S(6)} %copy.20.live, bf16[128,128]{1,0:T(8,128)(2,1)S(1)} %pad.5.stiff, f32[3072,1,128]{2,1,0:T(1,128)S(1)} %bitcast.10), custom_call_target="tpu_custom_call" | custom-call | tf_op jit(solution)/shard_map/pallas_call | solution.py:144
  119.2 0.0 copy-start.3
  119.2 1.0 copy-done.3
  120.2 1.0 slice_bitcast_fusion
  121.2 2.3 %copy.18 = f32[64,2048]{1,0:T(8,128)} copy(f32[64,2048]{0,1:T(8,128)} %slice_bitcast_fusion) | data formatting | bytes 1048576
  123.5 18.5 %shard_map.106 = (f32[256,128]{1,0:T(8,128)S(1)}, f32[256,128]{1,0:T(8,128)S(1)}) custom-call(f32[256,128]{1,0:T(8,128)S(1)} %get-tuple-element.46.send_low, f32[256,128]{1,0:T(8,128)S(1)} %get-tuple-element.47.send_high), custom_call_target="tpu_custom_call" | custom-call | tf_op jit(solution)/shard_map/pallas_call | solution.py:363
  142.0 0.0 copy-start.4
  142.0 1.2 copy-done.4
  143.2 3.8 %shard_map.107 = f32[2048,128]{1,0:T(8,128)S(1)} custom-call(s32[2,512]{1,0:T(2,128)S(1)} %bitcast.17, f32[2]{0:T(128)S(1)} %copy-done.8, f32[2048,128]{1,0:T(8,128)S(1)} %copy-done.4, f32[256,128]{1,0:T(8,128)S(1)} %get-tuple-element.48.from_low, f32[256,128]{1,0:T(8,128)S(1)} %get-tuple-element.49.from_high, f32[2048,128]{1,0:T(8,128)S(1)} %broadcast_in_dim.2.potential, ...), custom_call_target="tpu_custom_call" | custom-call | tf_op jit(solution)/shard_map/pallas_call | solution.py:253
  147.0 0.0 copy-start
  147.0 1.0 copy-done
  148.0 5.2 %all-gather.2.cloned.1.call-done = bf16[2048,256]{0,1:T(8,128)(2,1)} async-done(((bf16[2048,64]{0,1:T(8,128)(2,1)}), bf16[2048,256]{0,1:T(8,128)(2,1)}) %all-gather.2.cloned.1.call-update) | async-done | bytes 1048592 | tf_op jit(solution)/shard_map/all_gather | solution.py:477
  153.2 2.0 %convolution_multiply_fusion = f32[256,64]{0,1:T(8,128)S(1)} fusion(bf16[2048,256]{0,1:T(8,128)(2,1)} %all-gather.2.cloned.1.call-done, f32[2048,128]{1,0:T(8,128)} %copy-done), kind=kOutput, calls=%fused_computation | convolution fusion | flops 67125248 | bytes 1638400 | tf_op jit(solution)/shard_map/nw,nv->wv/dot_general | solution.py:488
  155.2 0.1 copy.17
  155.3 34.8 %shard_map.108 = f32[32,64]{1,0:T(8,128)S(1)} custom-call(f32[8,32,64]{2,1,0:T(8,128)S(1)} %bitcast.13), custom_call_target="tpu_custom_call" | custom-call | tf_op jit(solution)/shard_map/pallas_call | solution.py:431
  190.1 0.6 copy.21
  (1 shorter events, 0.0 us)
Async XLA Ops:
  7.2 3.1 %copy-start.6 = (s32[1,2,512]{2,1,0:T(2,128)S(1)}, s32[1,2,512]{2,1,0:T(2,128)}, u32[]{:S(2)}) copy-start(s32[1,2,512]{2,1,0:T(2,128)} %param.14) | copy-start | bytes 12292
  7.2 146.1 %all-gather.2.cloned.1.call-start = ((), (), s32[]{:S(2)}) async-start(), calls=%async_computation | async-start | bytes 1310720 | tf_op jit(solution)/shard_map/all_gather | solution.py:477
  12.4 4.0 %copy-start.5 = (s32[125,128]{1,0:T(8,128)S(1)}, s32[125,128]{1,0:T(8,128)}, u32[]{:S(2)}) copy-start(s32[125,128]{1,0:T(8,128)} %connect.5) | copy-start | bytes 192004
  12.4 4.0 %copy-start.7 = (f32[128]{0:T(128)S(1)}, f32[128]{0:T(128)}, u32[]{:S(2)}) copy-start(f32[128]{0:T(128)} %scale.5) | copy-start | bytes 1540
  16.4 16.2 %copy-start.9 = (f32[2048]{0:T(1024)S(1)}, f32[2048]{0:T(1024)}, u32[]{:S(2)}) copy-start(f32[2048]{0:T(1024)} %param.11) | copy-start | bytes 24580
  16.4 16.5 %copy-start.8 = (f32[2]{0:T(128)S(1)}, f32[2]{0:T(128)}, u32[]{:S(2)}) copy-start(f32[2]{0:T(128)} %window.5) | copy-start | bytes 28
  86.5 1.0 copy-start.1
  89.4 1.2 copy-start.2
  119.2 1.0 copy-start.3
  142.0 1.2 copy-start.4
  147.0 1.0 copy-start
Sparse Core Ops, SparseCore 0:
  89.5 63.6 all-gather.1

commit v4 on v3

--- a/solution.py
+++ b/solution.py
@@ -14,6 +14,7 @@
 LANES = 128
 HALF = LANES // 2
 WAYS = 4
+PAIRS = 2
 SHARED_WAYS = 2
 MIB = 1024 * 1024
 VMEM = pl.BlockSpec(memory_space=pltpu.VMEM)
@@ -75,38 +76,46 @@
     clear(sums)
 
     live_count = live[0]
-    pairs = (live_count + 1) // 2
-    last = capacity // 2 - 1
-
-    def cells_of(pair):
-        first = jnp.minimum(pair, last) * 2
-        return first, first + 1
-
-    def move(scatter_pair, p, gather_pair, x):
-        for begin in range(0, nodes, WAYS):
+    batch = 2 * PAIRS
+    steps = (live_count + batch - 1) // batch
+    last = capacity // batch - 1
+    turn_rows = WAYS // PAIRS
+    lanes = [slice(k * LANES, (k + 1) * LANES) for k in range(PAIRS)]
+
+    def first_cell(step):
+        return jnp.minimum(step, last) * batch
+
+    def move(scatter_step, p, gather_step, x):
+        done = first_cell(scatter_step)
+        begun = first_cell(gather_step)
+        for begin in range(0, nodes, turn_rows):
             todo = []
-            for way in range(min(WAYS, nodes - begin)):
-                j = begin + way
-                if p is not None:
-                    term = p[j : j + 1, :]
-                    for sums_of, cell in zip((lows, highs), cells_of(scatter_pair)):
-                        at = pl.ds(connect[j, cell], 1)
-                        todo.append((sums_of[way], at, sums_of[way][at, :] + term))
-                first, second = cells_of(gather_pair)
-                low = ext[connect[j, first]]
-                high = ext[connect[j, second]]
-                todo.append((x, pl.ds(j, 1), jnp.where(low_lanes, low, high)))
+            for row in range(min(turn_rows, nodes - begin)):
+                j = begin + row
+                for k in range(PAIRS):
+                    if p is not None:
+                        term = p[j : j + 1, lanes[k]]
+                        for side, sums_of in enumerate((lows, highs)):
+                            total = sums_of[row * PAIRS + k]
+                            at = pl.ds(connect[j, done + 2 * k + side], 1)
+                            todo.append((total, (at, slice(None)), total[at, :] + term))
+                    low = ext[connect[j, begun + 2 * k]]
+                    high = ext[connect[j, begun + 2 * k + 1]]
+                    todo.append((x, (pl.ds(j, 1), lanes[k]), jnp.where(low_lanes, low, high)))
             for ref, at, value in todo:
-                ref[at, :] = value
-
-    def multiply(pair, x, p):
-        first, second = cells_of(pair)
-        low = jnp.where(pair * 2 < live_count, scale[first], 0.0)
-        high = jnp.where(pair * 2 + 1 < live_count, scale[second], 0.0)
-        weight = jnp.where(low_lanes, low, high)
-        p[...] = weight * jnp.dot(
+                ref[at] = value
+
+    def multiply(step, x, p):
+        cell = first_cell(step)
+        weights = [
+            jnp.where(step * batch + k < live_count, scale[cell + k], 0.0) for k in range(batch)
+        ]
+        product = jnp.dot(
             stiff[...], x[...].astype(jnp.bfloat16), preferred_element_type=jnp.float32
         )
+        for k in range(PAIRS):
+            weight = jnp.where(low_lanes, weights[2 * k], weights[2 * k + 1])
+            p[:, lanes[k]] = weight * product[:, lanes[k]]
 
     x0[...] = jnp.zeros_like(x0)
     x1[...] = jnp.zeros_like(x1)
@@ -114,13 +123,13 @@
     multiply(0, x0, p0)
     move(0, None, 1, x1)
 
-    @pl.loop(0, (pairs + 1) // 2)
+    @pl.loop(0, (steps + 1) // 2)
     def _(turn):
-        pair = turn * 2
-        multiply(pair + 1, x1, p1)
-        move(pair, p0, pair + 2, x0)
-        multiply(pair + 2, x0, p0)
-        move(pair + 1, p1, pair + 3, x1)
+        step = turn * 2
+        multiply(step + 1, x1, p1)
+        move(step, p0, step + 2, x0)
+        multiply(step + 2, x0, p0)
+        move(step + 1, p1, step + 3, x1)
 
     def total(at):
         both = jnp.where(low_lanes, sum_of(lows, at), sum_of(highs, at))
@@ -138,6 +147,7 @@
 
 def cell_sums(ext, node_dev, stiff, connect, scale, live):
     nodes, capacity = connect.shape
+    assert capacity % (2 * PAIRS) == 0
     depth = stiff.shape[0]
     rows = ext.shape[0]
     half = (rows - node_dev) // 4
@@ -147,7 +157,7 @@
         + [jax.ShapeDtypeStruct((half, LANES), jnp.float32)] * 2,
         in_specs=[SMEM, SMEM, SMEM] + [VMEM] * 2,
         out_specs=[VMEM] * 3,
-        scratch_shapes=[pltpu.VMEM((depth, LANES), jnp.float32)] * 4
+        scratch_shapes=[pltpu.VMEM((depth, PAIRS * LANES), jnp.float32)] * 4
         + [pltpu.VMEM((rows, LANES), jnp.float32)] * (2 * WAYS),
         compiler_params=pltpu.CompilerParams(vmem_limit_bytes=24 * MIB),
     )(connect, scale, live, stiff, ext.reshape(rows, 1, LANES))
@@ -190,7 +200,7 @@
 
 
 def assemble_kernel(stage, shared, window, totals, from_low, from_high, potential, before, start, *refs):
-    outs = {"first": 3, "second": 4, "third": 1}[stage]
+    outs = {"first": 3, "second": 6, "third": 1}[stage]
     out, scratch = refs[:outs], refs[outs:]
     sums, scratch = scratch[: 4 * SHARED_WAYS], scratch[4 * SHARED_WAYS :]
     half = from_low.shape[0]
@@ -230,9 +240,12 @@
                 2.0 * sigma_two / half_width
             ) - sigma_one * sigma_two * start[at, :]
             out[3][at, :] = filtered
+            turned = filtered.T[:HALF, :]
+            out[4][:, at] = turned
+            out[5][:, at] = turned.astype(jnp.bfloat16)
             out[0][at, :] = filtered.astype(jnp.bfloat16).astype(jnp.float32)
         else:
-            out[0][at, :] = applied
+            out[0][at, :] = applied[:, :HALF].astype(jnp.bfloat16)
 
     chunks(totals.shape[0], pointwise)
     if stage != "third":
@@ -245,10 +258,18 @@
     half = from_low.shape[0]
     whole = jax.ShapeDtypeStruct(totals.shape, jnp.float32)
     packed = jax.ShapeDtypeStruct((half, LANES), jnp.bfloat16)
+    rows = totals.shape[0]
     out_shape = {
         "first": [whole, packed, packed],
-        "second": [whole, packed, packed, whole],
-        "third": [whole],
+        "second": [
+            whole,
+            packed,
+            packed,
+            whole,
+            jax.ShapeDtypeStruct((HALF, rows), jnp.float32),
+            jax.ShapeDtypeStruct((HALF, rows), jnp.bfloat16),
+        ],
+        "third": [jax.ShapeDtypeStruct((rows, HALF), jnp.bfloat16)],
     }[stage]
     return pl.pallas_call(
         functools.partial(assemble_kernel, stage),
@@ -470,12 +491,11 @@
         start,
         start,
     )
-    second, send_low, send_high, filtered = assemble(
+    second, send_low, send_high, filtered, filtered_rows, wave_rows = assemble(
         "second", lists, window, *totals_of(first, *sends), potential_wide, first, start
     )
-    wave_rounded = second[:, :columns].astype(jnp.bfloat16)
-    gathered = lax.all_gather(wave_rounded, "bands", axis=1, tiled=True)
-    (applied,) = assemble(
+    gathered = lax.all_gather(wave_rows, "bands", axis=0, tiled=True)
+    (apply_rounded,) = assemble(
         "third",
         lists,
         window,
@@ -484,12 +504,11 @@
         filtered,
         start,
     )
-    apply_rounded = applied[:, :columns].astype(jnp.bfloat16)
     partial_value = jnp.einsum(
-        "nw,nv->wv", gathered, apply_rounded, preferred_element_type=jnp.float32
+        "wn,nv->wv", gathered, apply_rounded, preferred_element_type=jnp.float32
     ) * (1.0 / (node_dev * count))
     projected = reduce_parts(partial_value.reshape(count, -1, columns), 2)
-    return (filtered[:, :columns].T, projected)
+    return (filtered_rows, projected)
 
 
 def solution(mesh):

time: 200 us -> 203 us (1.015)
  Pallas kernels: 160 us -> 182 us
  local copies, waits for them, and re-layouts: 13.8 us -> 3.28 us
  waiting for transfers between devices: 5.26 us -> 0.04 us
    pallas_call x6, Pallas kernels: 77.2 us -> 120 us  [exchange_call(): pl.pallas_call(functools.partial(kernel, lax.axis_size('cells')), out_sha...]
    pallas_call x1, Pallas kernels: 34.8 us -> 8.09 us  [reduce_parts(): pl.pallas_call(functools.partial(reduce_kernel, count), out_shape=jax.Sha...]
    unnamed x23 -> x18, local copies, waits for them, and re-layouts: 9.54 us -> 2.85 us
    all_gather x1, waiting for transfers between devices: 5.25 us -> 0.02 us  [local(): gathered = lax.all_gather(wave_rows, 'bands', axis=0, tiled=True)]
    pallas_call x3, Pallas kernels: 31.6 us -> 35.4 us  [cell_sums(): pl.pallas_call(functools.partial(cell_kernel, nodes, capacity), out_shape...]
    slice x2 -> x0, local copies, waits for them, and re-layouts: 2.77 us -> none  [local(): wave_rounded = second[:, :columns].astype(jnp.bfloat16)]
  transfers between devices with their start and end apart: 1 -> 1, of which waited for: 1 -> 0; matrix products, arithmetic and copies ran while one was open for 2% -> 0% of each run, Pallas kernels for 26% -> 28%
where the time goes in v4:
time: 203 us; the launch traced here: 202 us
  Pallas kernels  182 us (90%)
  between operations  14.9 us (7%)
  local copies, waits for them, and re-layouts  3.28 us (2%)
    pallas_call x6, Pallas kernels, exchange_call(): pl.pallas_call(functools.partial(kernel, lax.axis_size('cells')), out_sha...  120 us
    pallas_call x3, Pallas kernels, cell_sums(): pl.pallas_call(functools.partial(cell_kernel, nodes, capacity), out_shape...  35.4 us
    pallas_call x3, Pallas kernels, assemble(): pl.pallas_call(functools.partial(assemble_kernel, stage), out_shape=out_s...  16 us
    pallas_call x1, Pallas kernels, reduce_parts(): pl.pallas_call(functools.partial(reduce_kernel, count), out_shape=jax.Sha...  8.09 us
  transfers between devices with their start and end apart: 1, of which 0 were waited for; matrix products, arithmetic and copies ran while one was open for 0% of the time, Pallas kernels for 28%

profile of v4, /device:TPU:0, one launch (start us, length us, event | category | flops | bytes accessed | tf_op | source)
XLA Modules:
  0.0 202.1 jit_solution(8487959278060361793)
XLA Ops:
  7.2 0.0 copy-start.6
  7.2 0.0 copy-start.3
  7.2 0.0 all-gather.2.cloned.1.call-start
  7.2 1.2 copy.10
  8.5 0.3 convert_bitcast_fusion.wide.own.before.start
  8.7 0.0 copy-done.6
  9.4 0.0 copy-done.3
  9.4 2.2 %shard_map.95 = (bf16[256,128]{1,0:T(8,128)(2,1)S(1)}, bf16[256,128]{1,0:T(8,128)(2,1)S(1)}) custom-call(s32[2,512]{1,0:T(2,128)S(1)} %bitcast.13, f32[2048,128]{1,0:T(8,128)S(1)} %convert_bitcast_fusion.wide.own.before.start), custom_call_target="tpu_custom_call" | custom-call | tf_op jit(solution)/shard_map/pallas_call | solution.py:192
  11.6 0.0 copy-start.2
  11.6 0.0 copy-start.4
  11.6 4.0 %shard_map.96 = f32[3072,128]{1,0:T(8,128)S(1)} custom-call(f32[2048,128]{1,0:T(8,128)S(1)} %convert_bitcast_fusion.wide.own.before.start, bf16[256,128]{1,0:T(8,128)(2,1)S(1)} %get-tuple-element.28.send_low, bf16[256,128]{1,0:T(8,128)(2,1)S(1)} %get-tuple-element.29.send_high), custom_call_target="tpu_custom_call" | custom-call | tf_op jit(solution)/shard_map/pallas_call | solution.py:384
  15.6 0.0 copy-start.7
  15.6 0.0 copy-start.5
  15.6 0.0 copy-done.2
  15.7 0.0 copy-done.4
  15.7 11.7 %shard_map.97 = (f32[2048,128]{1,0:T(8,128)S(1)}, f32[256,128]{1,0:T(8,128)S(1)}, f32[256,128]{1,0:T(8,128)S(1)}) custom-call(s32[125,128]{1,0:T(8,128)S(1)} %copy-done.2, f32[128]{0:T(128)S(1)} %copy-done.4, s32[1]{0:T(128)S(6)} %copy.14.live, bf16[128,128]{1,0:T(8,128)(2,1)S(1)} %pad.5.stiff, f32[3072,1,128]{2,1,0:T(1,128)S(1)} %bitcast.9), custom_call_target="tpu_custom_call" | custom-call | tf_op jit(solution)/shard_map/pallas_call | solution.py:154
  27.4 34.7 %shard_map.98 = (f32[256,128]{1,0:T(8,128)S(1)}, f32[256,128]{1,0:T(8,128)S(1)}) custom-call(f32[256,128]{1,0:T(8,128)S(1)} %get-tuple-element.31.send_low, f32[256,128]{1,0:T(8,128)S(1)} %get-tuple-element.32.send_high), custom_call_target="tpu_custom_call" | custom-call | tf_op jit(solution)/shard_map/pallas_call | solution.py:384
  62.1 0.0 copy-done.7
  62.1 0.3 broadcast_in_dim.2.potential
  62.4 0.0 copy-done.5
  62.4 5.5 %shard_map.99 = (f32[2048,128]{1,0:T(8,128)S(1)}, bf16[256,128]{1,0:T(8,128)(2,1)S(1)}, bf16[256,128]{1,0:T(8,128)(2,1)S(1)}) custom-call(s32[2,512]{1,0:T(2,128)S(1)} %bitcast.14, f32[2]{0:T(128)S(1)} %copy-done.5, f32[2048,128]{1,0:T(8,128)S(1)} %get-tuple-element.30.totals, f32[256,128]{1,0:T(8,128)S(1)} %get-tuple-element.33.from_low, ...), custom_call_target="tpu_custom_call" | custom-call | tf_op jit(solution)/shard_map/pallas_call | solution.py:274
  67.9 4.5 %shard_map.100 = f32[3072,128]{1,0:T(8,128)S(1)} custom-call(f32[2048,128]{1,0:T(8,128)S(1)} %get-tuple-element.35.own.before, bf16[256,128]{1,0:T(8,128)(2,1)S(1)} %get-tuple-element.36.send_low, bf16[256,128]{1,0:T(8,128)(2,1)S(1)} %get-tuple-element.37.send_high), custom_call_target="tpu_custom_call" | custom-call | tf_op jit(solution)/shard_map/pallas_call | solution.py:384
  72.4 11.7 %shard_map.101 = (f32[2048,128]{1,0:T(8,128)S(1)}, f32[256,128]{1,0:T(8,128)S(1)}, f32[256,128]{1,0:T(8,128)S(1)}) custom-call(s32[125,128]{1,0:T(8,128)S(1)} %copy-done.2, f32[128]{0:T(128)S(1)} %copy-done.4, s32[1]{0:T(128)S(6)} %copy.14.live, bf16[128,128]{1,0:T(8,128)(2,1)S(1)} %pad.5.stiff, f32[3072,1,128]{2,1,0:T(1,128)S(1)} %bitcast.11), custom_call_target="tpu_custom_call" | custom-call | tf_op jit(solution)/shard_map/pallas_call | solution.py:154
  84.2 36.2 %shard_map.102 = (f32[256,128]{1,0:T(8,128)S(1)}, f32[256,128]{1,0:T(8,128)S(1)}) custom-call(f32[256,128]{1,0:T(8,128)S(1)} %get-tuple-element.39.send_low, f32[256,128]{1,0:T(8,128)S(1)} %get-tuple-element.40.send_high), custom_call_target="tpu_custom_call" | custom-call | tf_op jit(solution)/shard_map/pallas_call | solution.py:384
  120.4 6.7 %shard_map.103 = (f32[2048,128]{1,0:T(8,128)S(1)}, bf16[256,128]{1,0:T(8,128)(2,1)S(1)}, bf16[256,128]{1,0:T(8,128)(2,1)S(1)}, f32[2048,128]{1,0:T(8,128)S(1)}, ...) custom-call(s32[2,512]{1,0:T(2,128)S(1)} %bitcast.15, f32[2]{0:T(128)S(1)} %copy-done.5, ...), custom_call_target="tpu_custom_call" | custom-call | tf_op jit(solution)/shard_map/pallas_call | solution.py:274
  127.2 0.0 copy-start
  127.2 1.0 copy-done
  128.2 0.0 all-gather.2.cloned.1.call-update
  128.2 4.5 %shard_map.104 = f32[3072,128]{1,0:T(8,128)S(1)} custom-call(f32[2048,128]{1,0:T(8,128)S(1)} %get-tuple-element.45.own, bf16[256,128]{1,0:T(8,128)(2,1)S(1)} %get-tuple-element.46.send_low, bf16[256,128]{1,0:T(8,128)(2,1)S(1)} %get-tuple-element.47.send_high), custom_call_target="tpu_custom_call" | custom-call | tf_op jit(solution)/shard_map/pallas_call | solution.py:384
  132.7 0.0 copy-start.1
  132.7 11.9 %shard_map.105 = (f32[2048,128]{1,0:T(8,128)S(1)}, f32[256,128]{1,0:T(8,128)S(1)}, f32[256,128]{1,0:T(8,128)S(1)}) custom-call(s32[125,128]{1,0:T(8,128)S(1)} %copy-done.2, f32[128]{0:T(128)S(1)} %copy-done.4, s32[1]{0:T(128)S(6)} %copy.14.live, bf16[128,128]{1,0:T(8,128)(2,1)S(1)} %pad.5.stiff, f32[3072,1,128]{2,1,0:T(1,128)S(1)} %bitcast.10), custom_call_target="tpu_custom_call" | custom-call | tf_op jit(solution)/shard_map/pallas_call | solution.py:154
  144.6 36.2 %shard_map.106 = (f32[256,128]{1,0:T(8,128)S(1)}, f32[256,128]{1,0:T(8,128)S(1)}) custom-call(f32[256,128]{1,0:T(8,128)S(1)} %get-tuple-element.49.send_low, f32[256,128]{1,0:T(8,128)S(1)} %get-tuple-element.50.send_high), custom_call_target="tpu_custom_call" | custom-call | tf_op jit(solution)/shard_map/pallas_call | solution.py:384
  180.9 0.0 copy-done.1
  180.9 3.8 %shard_map.107 = bf16[2048,64]{1,0:T(8,128)(2,1)S(1)} custom-call(s32[2,512]{1,0:T(2,128)S(1)} %bitcast.16, f32[2]{0:T(128)S(1)} %copy-done.5, f32[2048,128]{1,0:T(8,128)S(1)} %get-tuple-element.48.totals, f32[256,128]{1,0:T(8,128)S(1)} %get-tuple-element.51.from_low, f32[256,128]{1,0:T(8,128)S(1)} %get-tuple-element.52.from_high, ...), custom_call_target="tpu_custom_call" | custom-call | tf_op jit(solution)/shard_map/pallas_call | solution.py:274
  184.7 0.0 all-gather.2.cloned.1.call-done
  184.7 1.7 convolution_multiply_fusion
  186.4 0.1 copy.12
  186.5 8.1 %shard_map.108 = f32[32,64]{1,0:T(8,128)S(1)} custom-call(f32[8,32,64]{2,1,0:T(8,128)S(1)} %bitcast.12), custom_call_target="tpu_custom_call" | custom-call | tf_op jit(solution)/shard_map/pallas_call | solution.py:452
  194.6 0.6 copy.15
  (2 shorter events, 0.0 us)
Async XLA Ops:
  7.2 1.6 copy-start.6
  7.2 2.2 %copy-start.3 = (s32[1,2,512]{2,1,0:T(2,128)S(1)}, s32[1,2,512]{2,1,0:T(2,128)}, u32[]{:S(2)}) copy-start(s32[1,2,512]{2,1,0:T(2,128)} %param.14) | copy-start | bytes 12292
  7.2 177.5 %all-gather.2.cloned.1.call-start = ((), (), s32[]{:S(2)}) async-start(), calls=%async_computation | async-start | bytes 1310720 | tf_op jit(solution)/shard_map/all_gather | solution.py:497
  11.6 4.1 %copy-start.2 = (s32[125,128]{1,0:T(8,128)S(1)}, s32[125,128]{1,0:T(8,128)}, u32[]{:S(2)}) copy-start(s32[125,128]{1,0:T(8,128)} %connect.5) | copy-start | bytes 192004
  11.6 4.1 %copy-start.4 = (f32[128]{0:T(128)S(1)}, f32[128]{0:T(128)}, u32[]{:S(2)}) copy-start(f32[128]{0:T(128)} %scale.5) | copy-start | bytes 1540
  15.6 46.5 %copy-start.7 = (f32[2048]{0:T(1024)S(1)}, f32[2048]{0:T(1024)}, u32[]{:S(2)}) copy-start(f32[2048]{0:T(1024)} %param.11) | copy-start | bytes 24580
  15.6 46.8 %copy-start.5 = (f32[2]{0:T(128)S(1)}, f32[2]{0:T(128)}, u32[]{:S(2)}) copy-start(f32[2]{0:T(128)} %window.5) | copy-start | bytes 28
  127.2 1.0 copy-start
  132.7 48.2 %copy-start.1 = (f32[2048,128]{1,0:T(8,128)S(1)}, f32[2048,128]{1,0:T(8,128)}, u32[]{:S(2)}) copy-start(f32[2048,128]{1,0:T(8,128)} %copy-done) | copy-start | bytes 3145732
Sparse Core Ops, SparseCore 0:
  128.3 30.3 all-gather.1

commit v5 on v4

--- a/solution.py
+++ b/solution.py
@@ -14,7 +14,7 @@
 LANES = 128
 HALF = LANES // 2
 WAYS = 4
-PAIRS = 2
+TRIP_ROWS = 64
 SHARED_WAYS = 2
 MIB = 1024 * 1024
 VMEM = pl.BlockSpec(memory_space=pltpu.VMEM)
@@ -53,7 +53,6 @@
 
 
 def cell_kernel(
-    nodes,
     capacity,
     connect,
     scale,
@@ -63,10 +62,8 @@
     out,
     out_low,
     out_high,
-    x0,
-    x1,
-    p0,
-    p1,
+    x,
+    p,
     *sums,
 ):
     lows, highs = sums[:WAYS], sums[WAYS:]
@@ -76,60 +73,50 @@
     clear(sums)
 
     live_count = live[0]
-    batch = 2 * PAIRS
-    steps = (live_count + batch - 1) // batch
-    last = capacity // batch - 1
-    turn_rows = WAYS // PAIRS
-    lanes = [slice(k * LANES, (k + 1) * LANES) for k in range(PAIRS)]
-
-    def first_cell(step):
-        return jnp.minimum(step, last) * batch
-
-    def move(scatter_step, p, gather_step, x):
-        done = first_cell(scatter_step)
-        begun = first_cell(gather_step)
-        for begin in range(0, nodes, turn_rows):
-            todo = []
-            for row in range(min(turn_rows, nodes - begin)):
-                j = begin + row
-                for k in range(PAIRS):
-                    if p is not None:
-                        term = p[j : j + 1, lanes[k]]
-                        for side, sums_of in enumerate((lows, highs)):
-                            total = sums_of[row * PAIRS + k]
-                            at = pl.ds(connect[j, done + 2 * k + side], 1)
-                            todo.append((total, (at, slice(None)), total[at, :] + term))
-                    low = ext[connect[j, begun + 2 * k]]
-                    high = ext[connect[j, begun + 2 * k + 1]]
-                    todo.append((x, (pl.ds(j, 1), lanes[k]), jnp.where(low_lanes, low, high)))
-            for ref, at, value in todo:
-                ref[at] = value
-
-    def multiply(step, x, p):
-        cell = first_cell(step)
-        weights = [
-            jnp.where(step * batch + k < live_count, scale[cell + k], 0.0) for k in range(batch)
-        ]
-        product = jnp.dot(
-            stiff[...], x[...].astype(jnp.bfloat16), preferred_element_type=jnp.float32
-        )
-        for k in range(PAIRS):
-            weight = jnp.where(low_lanes, weights[2 * k], weights[2 * k + 1])
-            p[:, lanes[k]] = weight * product[:, lanes[k]]
-
-    x0[...] = jnp.zeros_like(x0)
-    x1[...] = jnp.zeros_like(x1)
-    move(0, None, 0, x0)
-    multiply(0, x0, p0)
-    move(0, None, 1, x1)
-
-    @pl.loop(0, (steps + 1) // 2)
-    def _(turn):
-        step = turn * 2
-        multiply(step + 1, x1, p1)
-        move(step, p0, step + 2, x0)
-        multiply(step + 2, x0, p0)
-        move(step + 1, p1, step + 3, x1)
+    pairs = (live_count + 1) // 2
+    last = capacity // 2 - 1
+    depth = stiff.shape[0]
+    x[...] = jnp.zeros_like(x)
+    p[...] = jnp.zeros_like(p)
+
+    def first_cell(pair):
+        return jnp.clip(pair, 0, last) * 2
+
+    @pl.loop(0, pairs + 2)
+    def _(step):
+        now = lax.rem(step, 2)
+        other = 1 - now
+        done = first_cell(step - 2)
+        middle = first_cell(step - 1)
+        begun = first_cell(step)
+        weight = jnp.where(
+            low_lanes,
+            jnp.where(step * 2 - 2 < live_count, scale[middle], 0.0),
+            jnp.where(step * 2 - 1 < live_count, scale[middle + 1], 0.0),
+        )
+
+        @pl.loop(0, depth // TRIP_ROWS)
+        def _(trip):
+            base = pl.multiple_of(trip * TRIP_ROWS, TRIP_ROWS)
+            block = pl.ds(base, TRIP_ROWS)
+            product = weight * jnp.dot(
+                stiff[block, :], x[other].astype(jnp.bfloat16), preferred_element_type=jnp.float32
+            )
+            for begin in range(0, TRIP_ROWS, WAYS):
+                todo = []
+                for way in range(WAYS):
+                    j = base + begin + way
+                    term = p[now, pl.ds(j, 1), :]
+                    for total, cell in ((lows[way], done), (highs[way], done + 1)):
+                        at = pl.ds(connect[j, cell], 1)
+                        todo.append((total, (at, slice(None)), total[at, :] + term))
+                    low = ext[connect[j, begun]]
+                    high = ext[connect[j, begun + 1]]
+                    value = jnp.where(low_lanes, low, high)
+                    todo.append((x, (now, pl.ds(j, 1), slice(None)), value))
+                for ref, at, value in todo:
+                    ref[at] = value
+            p[other, block, :] = product
 
     def total(at):
         both = jnp.where(low_lanes, sum_of(lows, at), sum_of(highs, at))
@@ -146,18 +133,18 @@
 
 
 def cell_sums(ext, node_dev, stiff, connect, scale, live):
-    nodes, capacity = connect.shape
-    assert capacity % (2 * PAIRS) == 0
+    capacity = connect.shape[1]
+    assert capacity % 2 == 0
     depth = stiff.shape[0]
     rows = ext.shape[0]
     half = (rows - node_dev) // 4
     return pl.pallas_call(
-        functools.partial(cell_kernel, nodes, capacity),
+        functools.partial(cell_kernel, capacity),
         out_shape=[jax.ShapeDtypeStruct((node_dev, LANES), jnp.float32)]
         + [jax.ShapeDtypeStruct((half, LANES), jnp.float32)] * 2,
         in_specs=[SMEM, SMEM, SMEM] + [VMEM] * 2,
         out_specs=[VMEM] * 3,
-        scratch_shapes=[pltpu.VMEM((depth, PAIRS * LANES), jnp.float32)] * 4
+        scratch_shapes=[pltpu.VMEM((2, depth, LANES), jnp.float32)] * 2
         + [pltpu.VMEM((rows, LANES), jnp.float32)] * (2 * WAYS),
         compiler_params=pltpu.CompilerParams(vmem_limit_bytes=24 * MIB),
     )(connect, scale, live, stiff, ext.reshape(rows, 1, LANES))
@@ -471,6 +458,7 @@
     nodes = connect.shape[0]
     depth = -(-nodes // LANES) * LANES
     stiff = jnp.pad(stiffness, ((0, depth - nodes), (0, depth - nodes))).astype(jnp.bfloat16)
+    connect = jnp.pad(connect, ((0, depth - nodes), (0, 0)))
     lists = shared[0]
     potential_wide = jnp.broadcast_to(potential[:, None], (node_dev, LANES))
     count = lax.axis_size("cells")

time: 203 us -> 273 us (1.34)
  Pallas kernels: 182 us -> 250 us
    pallas_call x3, Pallas kernels: 35.4 us -> 102 us  [cell_sums(): pl.pallas_call(functools.partial(cell_kernel, capacity), out_shape=[jax.S...]
    pallas_call x1, Pallas kernels: 8.09 us -> 41 us  [reduce_parts(): pl.pallas_call(functools.partial(reduce_kernel, count), out_shape=jax.Sha...]
    pallas_call x6, Pallas kernels: 120 us -> 88.2 us  [exchange_call(): pl.pallas_call(functools.partial(kernel, lax.axis_size('cells')), out_sha...]
  transfers between devices with their start and end apart: 1 -> 1, of which waited for: 0 -> 0; matrix products, arithmetic and copies ran while one was open for 0% -> 0% of each run, Pallas kernels for 28% -> 29%
where the time goes in v5:
time: 273 us; the launch traced here: 270 us
  Pallas kernels  250 us (92%)
  between operations  14.9 us (5%)
  local copies, waits for them, and re-layouts  3.29 us (1%)
    pallas_call x3, Pallas kernels, cell_sums(): pl.pallas_call(functools.partial(cell_kernel, capacity), out_shape=[jax.S...  102 us
    pallas_call x6, Pallas kernels, exchange_call(): pl.pallas_call(functools.partial(kernel, lax.axis_size('cells')), out_sha...  88.2 us
    pallas_call x1, Pallas kernels, reduce_parts(): pl.pallas_call(functools.partial(reduce_kernel, count), out_shape=jax.Sha...  41 us
    pallas_call x3, Pallas kernels, assemble(): pl.pallas_call(functools.partial(assemble_kernel, stage), out_shape=out_s...  16 us
  transfers between devices with their start and end apart: 1, of which 0 were waited for; matrix products, arithmetic and copies ran while one was open for 0% of the time, Pallas kernels for 29%

profile of v5, /device:TPU:0, one launch (start us, length us, event | category | flops | bytes accessed | tf_op | source)
XLA Modules:
  0.0 269.8 jit_solution(9147458972230828436)
XLA Ops:
  7.2 0.0 copy-start.5
  7.2 0.0 copy-start.2
  7.2 0.0 all-gather.2.cloned.1.call-start
  7.2 1.2 copy.10
  8.5 0.3 convert_bitcast_fusion.wide.own.before.start
  8.7 0.0 copy-done.5
  9.4 0.0 copy-done.2
  9.4 2.2 shard_map.95
  11.6 0.0 copy-start.6
  11.6 0.0 copy-start.3
  11.6 4.0 %shard_map.96 = f32[3072,128]{1,0:T(8,128)S(1)} custom-call(f32[2048,128]{1,0:T(8,128)S(1)} %convert_bitcast_fusion.wide.own.before.start, bf16[256,128]{1,0:T(8,128)(2,1)S(1)} %get-tuple-element.28.send_low, bf16[256,128]{1,0:T(8,128)(2,1)S(1)} %get-tuple-element.29.send_high), custom_call_target="tpu_custom_call" | custom-call | tf_op jit(solution)/shard_map/pallas_call | solution.py:371
  15.6 0.0 copy-start.7
  15.6 0.0 copy-done.6
  15.6 0.0 copy-start.4
  15.7 0.0 copy-done.3
  15.7 34.1 %shard_map.97 = (f32[2048,128]{1,0:T(8,128)S(1)}, f32[256,128]{1,0:T(8,128)S(1)}, f32[256,128]{1,0:T(8,128)S(1)}) custom-call(s32[128,128]{1,0:T(8,128)S(1)} %pad.9.connect, f32[128]{0:T(128)S(1)} %copy-done.3, s32[1]{0:T(128)S(6)} %copy.14.live, bf16[128,128]{1,0:T(8,128)(2,1)S(1)} %pad.10.stiff, f32[3072,1,128]{2,1,0:T(1,128)S(1)} %bitcast.9), custom_call_target="tpu_custom_call" | custom-call | tf_op jit(solution)/shard_map/pallas_call | solution.py:141
  49.7 2.3 shard_map.98
  52.1 0.0 copy-done.7
  52.1 0.3 broadcast_in_dim.2.potential
  52.4 0.0 copy-done.4
  52.4 5.5 %shard_map.99 = (f32[2048,128]{1,0:T(8,128)S(1)}, bf16[256,128]{1,0:T(8,128)(2,1)S(1)}, bf16[256,128]{1,0:T(8,128)(2,1)S(1)}) custom-call(s32[2,512]{1,0:T(2,128)S(1)} %bitcast.14, f32[2]{0:T(128)S(1)} %copy-done.4, f32[2048,128]{1,0:T(8,128)S(1)} %get-tuple-element.30.totals, f32[256,128]{1,0:T(8,128)S(1)} %get-tuple-element.33.from_low, ...), custom_call_target="tpu_custom_call" | custom-call | tf_op jit(solution)/shard_map/pallas_call | solution.py:261
  57.9 4.5 %shard_map.100 = f32[3072,128]{1,0:T(8,128)S(1)} custom-call(f32[2048,128]{1,0:T(8,128)S(1)} %get-tuple-element.35.own.before, bf16[256,128]{1,0:T(8,128)(2,1)S(1)} %get-tuple-element.36.send_low, bf16[256,128]{1,0:T(8,128)(2,1)S(1)} %get-tuple-element.37.send_high), custom_call_target="tpu_custom_call" | custom-call | tf_op jit(solution)/shard_map/pallas_call | solution.py:371
  62.4 34.1 %shard_map.101 = (f32[2048,128]{1,0:T(8,128)S(1)}, f32[256,128]{1,0:T(8,128)S(1)}, f32[256,128]{1,0:T(8,128)S(1)}) custom-call(s32[128,128]{1,0:T(8,128)S(1)} %pad.9.connect, f32[128]{0:T(128)S(1)} %copy-done.3, s32[1]{0:T(128)S(6)} %copy.14.live, bf16[128,128]{1,0:T(8,128)(2,1)S(1)} %pad.10.stiff, f32[3072,1,128]{2,1,0:T(1,128)S(1)} %bitcast.11), custom_call_target="tpu_custom_call" | custom-call | tf_op jit(solution)/shard_map/pallas_call | solution.py:141
  96.5 36.7 %shard_map.102 = (f32[256,128]{1,0:T(8,128)S(1)}, f32[256,128]{1,0:T(8,128)S(1)}) custom-call(f32[256,128]{1,0:T(8,128)S(1)} %get-tuple-element.39.send_low, f32[256,128]{1,0:T(8,128)S(1)} %get-tuple-element.40.send_high), custom_call_target="tpu_custom_call" | custom-call | tf_op jit(solution)/shard_map/pallas_call | solution.py:371
  133.1 6.7 %shard_map.103 = (f32[2048,128]{1,0:T(8,128)S(1)}, bf16[256,128]{1,0:T(8,128)(2,1)S(1)}, bf16[256,128]{1,0:T(8,128)(2,1)S(1)}, f32[2048,128]{1,0:T(8,128)S(1)}, ...) custom-call(s32[2,512]{1,0:T(2,128)S(1)} %bitcast.15, f32[2]{0:T(128)S(1)} %copy-done.4, ...), custom_call_target="tpu_custom_call" | custom-call | tf_op jit(solution)/shard_map/pallas_call | solution.py:261
  139.8 0.0 copy-start
  139.8 1.0 copy-done
  140.8 0.0 all-gather.2.cloned.1.call-update
  140.9 4.5 %shard_map.104 = f32[3072,128]{1,0:T(8,128)S(1)} custom-call(f32[2048,128]{1,0:T(8,128)S(1)} %get-tuple-element.45.own, bf16[256,128]{1,0:T(8,128)(2,1)S(1)} %get-tuple-element.46.send_low, bf16[256,128]{1,0:T(8,128)(2,1)S(1)} %get-tuple-element.47.send_high), custom_call_target="tpu_custom_call" | custom-call | tf_op jit(solution)/shard_map/pallas_call | solution.py:371
  145.4 0.0 copy-start.1
  145.4 34.1 %shard_map.105 = (f32[2048,128]{1,0:T(8,128)S(1)}, f32[256,128]{1,0:T(8,128)S(1)}, f32[256,128]{1,0:T(8,128)S(1)}) custom-call(s32[128,128]{1,0:T(8,128)S(1)} %pad.9.connect, f32[128]{0:T(128)S(1)} %copy-done.3, s32[1]{0:T(128)S(6)} %copy.14.live, bf16[128,128]{1,0:T(8,128)(2,1)S(1)} %pad.10.stiff, f32[3072,1,128]{2,1,0:T(1,128)S(1)} %bitcast.10), custom_call_target="tpu_custom_call" | custom-call | tf_op jit(solution)/shard_map/pallas_call | solution.py:141
  179.4 36.3 %shard_map.106 = (f32[256,128]{1,0:T(8,128)S(1)}, f32[256,128]{1,0:T(8,128)S(1)}) custom-call(f32[256,128]{1,0:T(8,128)S(1)} %get-tuple-element.49.send_low, f32[256,128]{1,0:T(8,128)S(1)} %get-tuple-element.50.send_high), custom_call_target="tpu_custom_call" | custom-call | tf_op jit(solution)/shard_map/pallas_call | solution.py:371
  215.7 0.0 copy-done.1
  215.7 3.8 %shard_map.107 = bf16[2048,64]{1,0:T(8,128)(2,1)S(1)} custom-call(s32[2,512]{1,0:T(2,128)S(1)} %bitcast.16, f32[2]{0:T(128)S(1)} %copy-done.4, f32[2048,128]{1,0:T(8,128)S(1)} %get-tuple-element.48.totals, f32[256,128]{1,0:T(8,128)S(1)} %get-tuple-element.51.from_low, f32[256,128]{1,0:T(8,128)S(1)} %get-tuple-element.52.from_high, ...), custom_call_target="tpu_custom_call" | custom-call | tf_op jit(solution)/shard_map/pallas_call | solution.py:261
  219.5 0.0 all-gather.2.cloned.1.call-done
  219.6 1.7 convolution_multiply_fusion
  221.3 0.1 copy.12
  221.4 41.0 %shard_map.108 = f32[32,64]{1,0:T(8,128)S(1)} custom-call(f32[8,32,64]{2,1,0:T(8,128)S(1)} %bitcast.12), custom_call_target="tpu_custom_call" | custom-call | tf_op jit(solution)/shard_map/pallas_call | solution.py:439
  262.3 0.6 copy.15
  (3 shorter events, 0.0 us)
Async XLA Ops:
  7.2 1.6 copy-start.5
  7.2 2.2 copy-start.2
  7.2 212.4 %all-gather.2.cloned.1.call-start = ((), (), s32[]{:S(2)}) async-start(), calls=%async_computation | async-start | bytes 1310720 | tf_op jit(solution)/shard_map/all_gather | solution.py:485
  11.6 4.0 %copy-start.6 = (s32[125,128]{1,0:T(8,128)S(1)}, s32[125,128]{1,0:T(8,128)}, u32[]{:S(2)}) copy-start(s32[125,128]{1,0:T(8,128)} %param.12) | copy-start | bytes 192004
  11.6 4.1 %copy-start.3 = (f32[128]{0:T(128)S(1)}, f32[128]{0:T(128)}, u32[]{:S(2)}) copy-start(f32[128]{0:T(128)} %scale.5) | copy-start | bytes 1540
  15.6 36.5 %copy-start.7 = (f32[2048]{0:T(1024)S(1)}, f32[2048]{0:T(1024)}, u32[]{:S(2)}) copy-start(f32[2048]{0:T(1024)} %param.11) | copy-start | bytes 24580
  15.6 36.8 %copy-start.4 = (f32[2]{0:T(128)S(1)}, f32[2]{0:T(128)}, u32[]{:S(2)}) copy-start(f32[2]{0:T(128)} %window.5) | copy-start | bytes 28
  139.8 1.0 copy-start
  145.4 70.4 %copy-start.1 = (f32[2048,128]{1,0:T(8,128)S(1)}, f32[2048,128]{1,0:T(8,128)}, u32[]{:S(2)}) copy-start(f32[2048,128]{1,0:T(8,128)} %copy-done) | copy-start | bytes 3145732
Sparse Core Ops, SparseCore 0:
  141.0 63.7 all-gather.1
